TPU v7x, 512 devices: a whole 4x8x8 slice. The times are simulated.
512 devices in a mesh: blk: 64 (over x, z_lo, y), uly: 8 (over z_hi, core).
Axes of the slice: x: 4, y: 8, z: 8 (z_hi: 4, z_lo: 2; z = z_hi * 2 + z_lo), core: 2. Of those that a mesh axis runs over, the one named last changes fastest.
Arguments:
- query_rows: bfloat16 [32768, 5120], P(('blk', 'uly')), may hold values from -6 to 6
- key_rows: bfloat16 [32768, 5120], P(('blk', 'uly')), may hold values from -6 to 6
- value_rows: bfloat16 [32768, 5120], P(('blk', 'uly')), may hold values from -6 to 6
- out_grad: bfloat16 [32768, 5120], P(('blk', 'uly')), may hold values from -96 to 96
- log_sums: bfloat16 [32768, 40], P(('blk', 'uly')), as said below
- deltas: bfloat16 [32768, 40], P(('blk', 'uly')), may hold values from -900 to 900
Outputs:
- grad_query: bfloat16 [32768, 5120], P(('blk', 'uly'))
- grad_key: bfloat16 [32768, 5120], P(('blk', 'uly'))
- grad_value: bfloat16 [32768, 5120], P(('blk', 'uly'))
Inputs may be any that keep to these rules, and one draw needn't show every extreme that they name: `log_sums`: each value lies within 1 of log(1024) + 0.5.
All inputs are finite; a program needn't handle non-finite values.
Results may differ from a plain program's by a relative error of at most 0.0058.
Values may be sent and summed in bfloat16 or wider, within the bound.
No kernel may reach another device: no remote copies, remote signals or barrier semaphores. Data moves between devices by JAX's collectives and lax.ppermute only.
A program may use at most 64 MiB of HBM per device.

v0:
```python
import jax
import jax.numpy as jnp
from jax import lax
from jax.sharding import PartitionSpec as P


def passed_along(value, axis, by):
    devices = lax.axis_size(axis)
    return lax.ppermute(value, axis, [(i, (i + by) % devices) for i in range(devices)])


def block_grads(qb, gb, lb, db, kb, vb, scale):
    f32 = jnp.float32
    score = jnp.einsum("qhd,khd->hqk", qb, kb, preferred_element_type=f32) * scale
    prob = jnp.exp(score - jnp.transpose(lb.astype(f32))[:, :, None])
    prob_low = prob.astype(jnp.bfloat16)
    grad_value = jnp.einsum("hqk,qhd->khd", prob_low, gb, preferred_element_type=f32)
    grad_prob = jnp.einsum("qhd,khd->hqk", gb, vb, preferred_element_type=f32)
    grad_score = (prob * (grad_prob - jnp.transpose(db.astype(f32))[:, :, None])).astype(
        jnp.bfloat16
    )
    grad_query = jnp.einsum("hqk,khd->qhd", grad_score, kb, preferred_element_type=f32) * scale
    grad_key = jnp.einsum("hqk,qhd->khd", grad_score, qb, preferred_element_type=f32) * scale
    return (grad_query, grad_key, grad_value)


def per_device(query_rows, key_rows, value_rows, out_grad, log_sums, deltas):
    heads_total = log_sums.shape[1]
    head_size = query_rows.shape[1] // heads_total
    scale = head_size ** (-0.5)
    queries, keys_mine, values_mine, grads_mine, sums_mine, delta_mine = (
        lax.all_to_all(query_rows, "uly", split_axis=1, concat_axis=0, tiled=True),
        lax.all_to_all(key_rows, "uly", split_axis=1, concat_axis=0, tiled=True),
        lax.all_to_all(value_rows, "uly", split_axis=1, concat_axis=0, tiled=True),
        lax.all_to_all(out_grad, "uly", split_axis=1, concat_axis=0, tiled=True),
        lax.all_to_all(log_sums, "uly", split_axis=1, concat_axis=0, tiled=True),
        lax.all_to_all(deltas, "uly", split_axis=1, concat_axis=0, tiled=True),
    )
    rows = queries.shape[0]
    local_heads = sums_mine.shape[1]
    shape3 = (rows, local_heads, head_size)
    queries = queries.reshape(shape3)
    keys_mine = keys_mine.reshape(shape3)
    values_mine = values_mine.reshape(shape3)
    grads_mine = grads_mine.reshape(shape3)
    own = block_grads(queries, grads_mine, sums_mine, delta_mine, keys_mine, values_mine, scale)
    keys_next, values_next = passed_along((keys_mine, values_mine), "blk", -1)
    cross = block_grads(queries, grads_mine, sums_mine, delta_mine, keys_next, values_next, scale)
    key_back, value_back = passed_along((cross[1], cross[2]), "blk", 1)
    grad_q = own[0] + cross[0]
    grad_k = own[1] + key_back
    grad_v = own[2] + value_back
    flat = (rows, local_heads * head_size)
    low_q = grad_q.astype(jnp.bfloat16).reshape(flat)
    low_k = grad_k.astype(jnp.bfloat16).reshape(flat)
    low_v = grad_v.astype(jnp.bfloat16).reshape(flat)
    out_q, out_k, out_v = (
        lax.all_to_all(low_q, "uly", split_axis=0, concat_axis=1, tiled=True),
        lax.all_to_all(low_k, "uly", split_axis=0, concat_axis=1, tiled=True),
        lax.all_to_all(low_v, "uly", split_axis=0, concat_axis=1, tiled=True),
    )
    return (out_q, out_k, out_v)


def solution(mesh):
    placed = (
        P(("blk", "uly"), None),
        P(("blk", "uly"), None),
        P(("blk", "uly"), None),
        P(("blk", "uly"), None),
        P(("blk", "uly"), None),
        P(("blk", "uly"), None),
    )
    return jax.shard_map(
        per_device,
        mesh=mesh,
        in_specs=placed,
        out_specs=(P(("blk", "uly"), None), P(("blk", "uly"), None), P(("blk", "uly"), None)),
        check_vma=False,
    )
```

profile of v0, /device:TPU:6, one launch (start us, length us, event | category | flops | bytes accessed | tf_op | source)
XLA Modules:
  0.0 298.7 jit_solution(14819714684129420937)
XLA Ops:
  0.6 0.8 all_to_all.116
  1.4 0.7 reshape.69
  2.1 10.3 %all-to-all-start.2 = ((bf16[8,2,160]{2,1,0:T(2,128)(2,1)}), bf16[8,2,160]{2,1,0:T(2,128)(2,1)S(1)}, u32[]{:S(2)}, u32[]{:S(2)}) async-start(bf16[8,2,160]{2,1,0:T(2,128)(2,1)} %reshape.69), calls=%async_computation.2 | async-start | bytes 16384 | tf_op jit(solution)/shard_map/all_to_all | solution.py:36
  12.4 0.7 all_to_all.124
  13.1 0.7 reshape.67
  13.8 6.3 %all-to-all-done.2 = bf16[8,2,160]{2,1,0:T(2,128)(2,1)S(1)} async-done(((bf16[8,2,160]{2,1,0:T(2,128)(2,1)}), bf16[8,2,160]{2,1,0:T(2,128)(2,1)S(1)}, u32[]{:S(2)}, u32[]{:S(2)}) %all-to-all-start.2) | async-done | bytes 5152 | tf_op jit(solution)/shard_map/all_to_all | solution.py:36
  20.1 3.3 %all-to-all-start.5 = ((bf16[8,2,160]{2,1,0:T(2,128)(2,1)}), bf16[8,2,160]{2,1,0:T(2,128)(2,1)S(1)}, u32[]{:S(2)}, u32[]{:S(2)}) async-start(bf16[8,2,160]{2,1,0:T(2,128)(2,1)} %reshape.67), calls=%async_computation.5 | async-start | bytes 16384 | tf_op jit(solution)/shard_map/all_to_all | solution.py:37
  23.5 0.0 copy-start.9
  23.5 2.1 copy.102
  25.6 5.6 %all-to-all-done.5 = bf16[8,2,160]{2,1,0:T(2,128)(2,1)S(1)} async-done(((bf16[8,2,160]{2,1,0:T(2,128)(2,1)}), bf16[8,2,160]{2,1,0:T(2,128)(2,1)S(1)}, u32[]{:S(2)}, u32[]{:S(2)}) %all-to-all-start.5) | async-done | bytes 5152 | tf_op jit(solution)/shard_map/all_to_all | solution.py:37
  31.1 3.5 %all-to-all-start = ((bf16[64,8,640]{2,0,1:T(8,128)(2,1)}), bf16[64,8,640]{2,0,1:T(8,128)(2,1)S(1)}, u32[]{:S(2)}, u32[]{:S(2)}) async-start(bf16[64,8,640]{2,0,1:T(8,128)(2,1)} %bitcast.76), calls=%async_computation | async-start | bytes 1310720 | tf_op jit(solution)/shard_map/all_to_all | solution.py:32
  34.7 0.0 copy-start.10
  34.7 0.9 copy.101
  35.6 20.2 %all-to-all-done = bf16[64,8,640]{2,0,1:T(8,128)(2,1)S(1)} async-done(((bf16[64,8,640]{2,0,1:T(8,128)(2,1)}), bf16[64,8,640]{2,0,1:T(8,128)(2,1)S(1)}, u32[]{:S(2)}, u32[]{:S(2)}) %all-to-all-start) | async-done | bytes 655392 | tf_op jit(solution)/shard_map/all_to_all | solution.py:32
  55.8 3.5 %all-to-all-start.1 = ((bf16[64,8,640]{2,0,1:T(8,128)(2,1)}), bf16[64,8,640]{2,0,1:T(8,128)(2,1)S(1)}, u32[]{:S(2)}, u32[]{:S(2)}) async-start(bf16[64,8,640]{2,0,1:T(8,128)(2,1)} %bitcast.75), calls=%async_computation.1 | async-start | bytes 1310720 | tf_op jit(solution)/shard_map/all_to_all | solution.py:33
  59.3 0.9 copy.99
  60.2 19.6 %all-to-all-done.1 = bf16[64,8,640]{2,0,1:T(8,128)(2,1)S(1)} async-done(((bf16[64,8,640]{2,0,1:T(8,128)(2,1)}), bf16[64,8,640]{2,0,1:T(8,128)(2,1)S(1)}, u32[]{:S(2)}, u32[]{:S(2)}) %all-to-all-start.1) | async-done | bytes 655392 | tf_op jit(solution)/shard_map/all_to_all | solution.py:33
  79.8 3.5 %all-to-all-start.4 = ((bf16[64,8,640]{2,0,1:T(8,128)(2,1)}), bf16[64,8,640]{2,0,1:T(8,128)(2,1)S(1)}, u32[]{:S(2)}, u32[]{:S(2)}) async-start(bf16[64,8,640]{2,0,1:T(8,128)(2,1)} %bitcast.73), calls=%async_computation.4 | async-start | bytes 1310720 | tf_op jit(solution)/shard_map/all_to_all | solution.py:34
  83.4 0.9 copy.100
  84.3 20.0 %all-to-all-done.4 = bf16[64,8,640]{2,0,1:T(8,128)(2,1)S(1)} async-done(((bf16[64,8,640]{2,0,1:T(8,128)(2,1)}), bf16[64,8,640]{2,0,1:T(8,128)(2,1)S(1)}, u32[]{:S(2)}, u32[]{:S(2)}) %all-to-all-start.4) | async-done | bytes 655392 | tf_op jit(solution)/shard_map/all_to_all | solution.py:34
  104.3 4.2 %all-to-all-start.3 = ((bf16[64,8,640]{2,0,1:T(8,128)(2,1)}), bf16[64,8,640]{2,0,1:T(8,128)(2,1)}, u32[]{:S(2)}, u32[]{:S(2)}) async-start(bf16[64,8,640]{2,0,1:T(8,128)(2,1)} %bitcast.74), calls=%async_computation.3 | async-start | bytes 1310720 | tf_op jit(solution)/shard_map/all_to_all | solution.py:35
  108.5 0.1 reshape.70
  108.6 0.1 reshape.65
  108.7 0.1 reshape.68
  108.8 0.1 reshape.66
  108.9 0.7 reshape.61
  109.6 0.7 reshape.62
  110.4 0.1 copy.42
  110.5 1.8 reshape.64
  112.3 0.9 copy.47
  113.2 16.0 %all-to-all-done.3 = bf16[64,8,640]{2,0,1:T(8,128)(2,1)} async-done(((bf16[64,8,640]{2,0,1:T(8,128)(2,1)}), bf16[64,8,640]{2,0,1:T(8,128)(2,1)}, u32[]{:S(2)}, u32[]{:S(2)}) %all-to-all-start.3) | async-done | bytes 655392 | tf_op jit(solution)/shard_map/all_to_all | solution.py:35
  129.2 2.6 reshape.63
  131.8 6.4 %collective-permute-start.1 = (bf16[512,5,128]{2,0,1:T(8,128)(2,1)}, bf16[512,5,128]{2,0,1:T(8,128)(2,1)S(1)}, u32[]{:S(2)}, u32[]{:S(2)}) collective-permute-start(bf16[512,5,128]{2,0,1:T(8,128)(2,1)} %copy.47), channel_id=1, source_target_pairs={{0,504},{8,0},{16,8},{24,16},{32,24},{40,32},{48,40},{56,48},{64,5... | collective-permute-start | bytes 1966088 | tf_op jit(solution)/shard_map/ppermute | solution.py:9
  138.2 3.3 %collective-permute-start = (bf16[512,5,128]{2,0,1:T(8,128)(2,1)S(1)}, bf16[512,5,128]{2,0,1:T(8,128)(2,1)S(1)}, u32[]{:S(2)}, u32[]{:S(2)}) collective-permute-start(bf16[512,5,128]{2,0,1:T(8,128)(2,1)S(1)} %copy.42), channel_id=1, source_target_pairs={{0,504},{8,0},{16,8},{24,16},{32,24},{40,32},{48,40},{56,48},{64,5... | collective-permute-start | bytes 1966088 | tf_op jit(solution)/shard_map/ppermute | solution.py:9
  141.4 0.8 fusion.39
  142.3 3.5 %multiply_convert_fusion.1 = bf16[5,512,512]{2,1,0:T(8,128)(2,1)S(1)} fusion(f32[5,512,512]{2,1,0:T(8,128)S(1)} %fusion.39, f32[5,512]{1,0:T(8,128)S(1)} %bitcast.93, f32[5,512]{1,0:T(8,128)S(1)} %bitcast.89, bf16[512,5,128]{2,0,1:T(8,128)(2,1)} %copy.47, bf16[512,5,128]{2,1,0:T(8,128)(2,1)S(1)} %copy-done.2), kind=kOutput, calls=%fused_computation.2 | convolution fusion | flops 342097920 | bytes 9195520 | tf_op jit(solution)/shard_map/qhd,khd->hqk/dot_general | solution.py:18
  145.8 18.9 %collective-permute-done = bf16[512,5,128]{2,0,1:T(8,128)(2,1)S(1)} collective-permute-done((bf16[512,5,128]{2,0,1:T(8,128)(2,1)S(1)}, bf16[512,5,128]{2,0,1:T(8,128)(2,1)S(1)}, u32[]{:S(2)}, u32[]{:S(2)}) %collective-permute-start) | collective-permute-done | bytes 655392 | tf_op jit(solution)/shard_map/ppermute | solution.py:9
  164.8 0.8 fusion.37
  165.6 1.7 multiply_convert_fusion
  167.3 0.7 copy-done
  168.0 2.2 fusion.16
  170.2 2.1 collective-permute-start.2
  172.3 0.8 fusion.41
  173.2 0.9 fusion.28
  174.0 1.4 copy.54
  175.5 2.6 all_to_all.126
  178.1 4.2 %all-to-all-start.6 = ((bf16[8,64,640]{2,1,0:T(8,128)(2,1)}), bf16[8,64,640]{2,1,0:T(8,128)(2,1)}, u32[]{:S(2)}, u32[]{:S(2)}) async-start(bf16[8,64,640]{2,1,0:T(8,128)(2,1)} %all_to_all.126), calls=%async_computation.6 | async-start | bytes 1310720 | tf_op jit(solution)/shard_map/all_to_all | solution.py:58
  182.3 5.6 %fusion.13 = f32[512,5,128]{2,0,1:T(8,128)} fusion(f32[5,512,512]{2,1,0:T(8,128)} %copy-done, f32[5,512]{1,0:T(8,128)S(1)} %bitcast.91, bf16[512,5,128]{2,1,0:T(8,128)(2,1)} %reshape.63), kind=kOutput, calls=%fused_computation.13 | convolution fusion | flops 339476480 | bytes 7219200 | tf_op jit(solution)/shard_map/hqk,qhd->khd/dot_general | solution.py:17
  187.9 2.6 collective-permute-start.3
  190.5 20.8 %collective-permute-done.2 = f32[512,5,128]{2,0,1:T(8,128)} collective-permute-done((f32[512,5,128]{2,0,1:T(8,128)}, f32[512,5,128]{2,0,1:T(8,128)}, u32[]{:S(2)}, u32[]{:S(2)}) %collective-permute-start.2) | collective-permute-done | bytes 1310752 | tf_op jit(solution)/shard_map/ppermute | solution.py:9
  211.3 2.4 fusion.27
  213.7 0.5 copy.60
  214.1 1.6 all_to_all.130
  215.8 29.9 %all-to-all-done.6 = bf16[8,64,640]{2,1,0:T(8,128)(2,1)} async-done(((bf16[8,64,640]{2,1,0:T(8,128)(2,1)}), bf16[8,64,640]{2,1,0:T(8,128)(2,1)}, u32[]{:S(2)}, u32[]{:S(2)}) %all-to-all-start.6) | async-done | bytes 655392 | tf_op jit(solution)/shard_map/all_to_all | solution.py:58
  245.6 7.0 %all-to-all-start.7 = ((bf16[8,64,640]{2,1,0:T(8,128)(2,1)}), bf16[8,64,640]{2,1,0:T(8,128)(2,1)S(1)}, u32[]{:S(2)}, u32[]{:S(2)}) async-start(bf16[8,64,640]{2,1,0:T(8,128)(2,1)} %all_to_all.130), calls=%async_computation.7 | async-start | bytes 1310720 | tf_op jit(solution)/shard_map/all_to_all | solution.py:59
  252.6 4.7 %fusion.23 = bf16[512,5,128]{2,0,1:T(8,128)(2,1)S(1)} fusion(f32[512,5,128]{2,0,1:T(8,128)} %collective-permute-done.3, f32[5,512,512]{2,1,0:T(8,128)} %copy-done.1, f32[5,512]{1,0:T(8,128)S(1)} %bitcast.92, bf16[512,5,128]{2,1,0:T(8,128)(2,1)S(1)} %copy-done.3), kind=kOutput, calls=%fused_computation.22 | convolution fusion | flops 340131840 | bytes 7874560 | tf_op jit(solution)/shard_map/hqk,qhd->khd/dot_general | solution.py:17
  257.3 0.5 copy.66
  257.8 1.6 all_to_all.134
  259.4 14.4 %all-to-all-done.7 = bf16[8,64,640]{2,1,0:T(8,128)(2,1)S(1)} async-done(((bf16[8,64,640]{2,1,0:T(8,128)(2,1)}), bf16[8,64,640]{2,1,0:T(8,128)(2,1)S(1)}, u32[]{:S(2)}, u32[]{:S(2)}) %all-to-all-start.7) | async-done | bytes 655392 | tf_op jit(solution)/shard_map/all_to_all | solution.py:59
  273.8 3.5 %all-to-all-start.8 = ((bf16[8,64,640]{2,1,0:T(8,128)(2,1)}), bf16[8,64,640]{2,1,0:T(8,128)(2,1)S(1)}, u32[]{:S(2)}, u32[]{:S(2)}) async-start(bf16[8,64,640]{2,1,0:T(8,128)(2,1)} %all_to_all.134), calls=%async_computation.8 | async-start | bytes 1310720 | tf_op jit(solution)/shard_map/all_to_all | solution.py:60
  277.3 2.0 copy.76
  279.3 0.9 copy.77
  280.2 17.6 %all-to-all-done.8 = bf16[8,64,640]{2,1,0:T(8,128)(2,1)S(1)} async-done(((bf16[8,64,640]{2,1,0:T(8,128)(2,1)}), bf16[8,64,640]{2,1,0:T(8,128)(2,1)S(1)}, u32[]{:S(2)}, u32[]{:S(2)}) %all-to-all-start.8) | async-done | bytes 655392 | tf_op jit(solution)/shard_map/all_to_all | solution.py:60
  297.8 0.9 copy.78
  (25 shorter events, 0.1 us)
Async XLA Ops:
  0.6 34.0 %copy-start.8 = (bf16[64,5120]{1,0:T(8,128)(2,1)S(1)}, bf16[64,5120]{1,0:T(8,128)(2,1)}, u32[]{:S(2)}) copy-start(bf16[64,5120]{1,0:T(8,128)(2,1)} %param.7) | copy-start | bytes 1966084
  2.1 18.0 %all-to-all-start.2 = ((bf16[8,2,160]{2,1,0:T(2,128)(2,1)}), bf16[8,2,160]{2,1,0:T(2,128)(2,1)S(1)}, u32[]{:S(2)}, u32[]{:S(2)}) async-start(bf16[8,2,160]{2,1,0:T(2,128)(2,1)} %reshape.69), calls=%async_computation.2 | async-start | bytes 16384 | tf_op jit(solution)/shard_map/all_to_all | solution.py:36
  20.1 11.0 %all-to-all-start.5 = ((bf16[8,2,160]{2,1,0:T(2,128)(2,1)}), bf16[8,2,160]{2,1,0:T(2,128)(2,1)S(1)}, u32[]{:S(2)}, u32[]{:S(2)}) async-start(bf16[8,2,160]{2,1,0:T(2,128)(2,1)} %reshape.67), calls=%async_computation.5 | async-start | bytes 16384 | tf_op jit(solution)/shard_map/all_to_all | solution.py:37
  23.5 35.8 %copy-start.9 = (bf16[64,5120]{1,0:T(8,128)(2,1)S(1)}, bf16[64,5120]{1,0:T(8,128)(2,1)}, u32[]{:S(2)}) copy-start(bf16[64,5120]{1,0:T(8,128)(2,1)} %param.8) | copy-start | bytes 1966084
  31.1 24.6 %all-to-all-start = ((bf16[64,8,640]{2,0,1:T(8,128)(2,1)}), bf16[64,8,640]{2,0,1:T(8,128)(2,1)S(1)}, u32[]{:S(2)}, u32[]{:S(2)}) async-start(bf16[64,8,640]{2,0,1:T(8,128)(2,1)} %bitcast.76), calls=%async_computation | async-start | bytes 1310720 | tf_op jit(solution)/shard_map/all_to_all | solution.py:32
  34.7 48.7 %copy-start.10 = (bf16[64,5120]{1,0:T(8,128)(2,1)S(1)}, bf16[64,5120]{1,0:T(8,128)(2,1)}, u32[]{:S(2)}) copy-start(bf16[64,5120]{1,0:T(8,128)(2,1)} %param.9) | copy-start | bytes 1966084
  55.8 24.0 %all-to-all-start.1 = ((bf16[64,8,640]{2,0,1:T(8,128)(2,1)}), bf16[64,8,640]{2,0,1:T(8,128)(2,1)S(1)}, u32[]{:S(2)}, u32[]{:S(2)}) async-start(bf16[64,8,640]{2,0,1:T(8,128)(2,1)} %bitcast.75), calls=%async_computation.1 | async-start | bytes 1310720 | tf_op jit(solution)/shard_map/all_to_all | solution.py:33
  79.8 24.5 %all-to-all-start.4 = ((bf16[64,8,640]{2,0,1:T(8,128)(2,1)}), bf16[64,8,640]{2,0,1:T(8,128)(2,1)S(1)}, u32[]{:S(2)}, u32[]{:S(2)}) async-start(bf16[64,8,640]{2,0,1:T(8,128)(2,1)} %bitcast.73), calls=%async_computation.4 | async-start | bytes 1310720 | tf_op jit(solution)/shard_map/all_to_all | solution.py:34
  104.3 4.6 %copy-start.7 = (bf16[64,8,640]{2,0,1:T(8,128)(2,1)}, bf16[64,8,640]{2,0,1:T(8,128)(2,1)S(1)}, u32[]{:S(2)}) copy-start(bf16[64,8,640]{2,0,1:T(8,128)(2,1)S(1)} %all-to-all-done.4) | copy-start | bytes 1966084
  104.3 24.9 %all-to-all-start.3 = ((bf16[64,8,640]{2,0,1:T(8,128)(2,1)}), bf16[64,8,640]{2,0,1:T(8,128)(2,1)}, u32[]{:S(2)}, u32[]{:S(2)}) async-start(bf16[64,8,640]{2,0,1:T(8,128)(2,1)} %bitcast.74), calls=%async_computation.3 | async-start | bytes 1310720 | tf_op jit(solution)/shard_map/all_to_all | solution.py:35
  109.6 31.8 %copy-start.4 = (bf16[512,5,128]{2,1,0:T(8,128)(2,1)}, bf16[512,5,128]{2,1,0:T(8,128)(2,1)S(1)}, u32[]{:S(2)}) copy-start(bf16[512,5,128]{2,1,0:T(8,128)(2,1)S(1)} %reshape.61) | copy-start | bytes 1966084
  131.8 10.5 %copy-start.2 = (bf16[512,5,128]{2,1,0:T(8,128)(2,1)S(1)}, bf16[512,5,128]{2,1,0:T(8,128)(2,1)}, u32[]{:S(2)}) copy-start(bf16[512,5,128]{2,1,0:T(8,128)(2,1)} %reshape.63) | copy-start | bytes 1966084
  131.8 33.8 %collective-permute-start.1 = (bf16[512,5,128]{2,0,1:T(8,128)(2,1)}, bf16[512,5,128]{2,0,1:T(8,128)(2,1)S(1)}, u32[]{:S(2)}, u32[]{:S(2)}) collective-permute-start(bf16[512,5,128]{2,0,1:T(8,128)(2,1)} %copy.47), channel_id=1, source_target_pairs={{0,504},{8,0},{16,8},{24,16},{32,24},{40,32},{48,40},{56,48},{64,5... | collective-permute-start | bytes 1966088 | tf_op jit(solution)/shard_map/ppermute | solution.py:9
  138.2 26.6 %collective-permute-start = (bf16[512,5,128]{2,0,1:T(8,128)(2,1)S(1)}, bf16[512,5,128]{2,0,1:T(8,128)(2,1)S(1)}, u32[]{:S(2)}, u32[]{:S(2)}) collective-permute-start(bf16[512,5,128]{2,0,1:T(8,128)(2,1)S(1)} %copy.42), channel_id=1, source_target_pairs={{0,504},{8,0},{16,8},{24,16},{32,24},{40,32},{48,40},{56,48},{64,5... | collective-permute-start | bytes 1966088 | tf_op jit(solution)/shard_map/ppermute | solution.py:9
  142.3 3.5 %copy-start.1 = (f32[5,512,512]{2,1,0:T(8,128)}, f32[5,512,512]{2,1,0:T(8,128)S(1)}, u32[]{:S(2)}) copy-start(f32[5,512,512]{2,1,0:T(8,128)S(1)} %fusion.39) | copy-start | bytes 15728644
  142.3 22.5 %copy-start.5 = (bf16[512,5,128]{2,1,0:T(8,128)(2,1)S(1)}, bf16[512,5,128]{2,1,0:T(8,128)(2,1)}, u32[]{:S(2)}) copy-start(bf16[512,5,128]{2,1,0:T(8,128)(2,1)} %copy-done.4) | copy-start | bytes 1966084
  165.6 2.4 copy-start
  170.2 41.1 %collective-permute-start.2 = (f32[512,5,128]{2,0,1:T(8,128)}, f32[512,5,128]{2,0,1:T(8,128)}, u32[]{:S(2)}, u32[]{:S(2)}) collective-permute-start(f32[512,5,128]{2,0,1:T(8,128)} %fusion.16), channel_id=1, source_target_pairs={{0,8},{8,16},{16,24},{24,32},{32,40},{40,48},{48,56},{56,64},{64,7... | collective-permute-start | bytes 3932168 | tf_op jit(solution)/shard_map/ppermute | solution.py:9
  178.1 67.5 %all-to-all-start.6 = ((bf16[8,64,640]{2,1,0:T(8,128)(2,1)}), bf16[8,64,640]{2,1,0:T(8,128)(2,1)}, u32[]{:S(2)}, u32[]{:S(2)}) async-start(bf16[8,64,640]{2,1,0:T(8,128)(2,1)} %all_to_all.126), calls=%async_computation.6 | async-start | bytes 1310720 | tf_op jit(solution)/shard_map/all_to_all | solution.py:58
  182.3 29.0 %copy-start.6 = (bf16[512,5,128]{2,1,0:T(8,128)(2,1)S(1)}, bf16[512,5,128]{2,1,0:T(8,128)(2,1)}, u32[]{:S(2)}) copy-start(bf16[512,5,128]{2,1,0:T(8,128)(2,1)} %copy-done.4) | copy-start | bytes 1966084
  187.9 64.7 %collective-permute-start.3 = (f32[512,5,128]{2,0,1:T(8,128)}, f32[512,5,128]{2,0,1:T(8,128)}, u32[]{:S(2)}, u32[]{:S(2)}) collective-permute-start(f32[512,5,128]{2,0,1:T(8,128)} %fusion.13), channel_id=1, source_target_pairs={{0,8},{8,16},{16,24},{24,32},{32,40},{40,48},{48,56},{56,64},{64,7... | collective-permute-start | bytes 3932168 | tf_op jit(solution)/shard_map/ppermute | solution.py:9
  213.7 38.9 %copy-start.3 = (bf16[512,5,128]{2,1,0:T(8,128)(2,1)S(1)}, bf16[512,5,128]{2,1,0:T(8,128)(2,1)}, u32[]{:S(2)}) copy-start(bf16[512,5,128]{2,1,0:T(8,128)(2,1)} %reshape.63) | copy-start | bytes 1966084
  245.6 28.2 %all-to-all-start.7 = ((bf16[8,64,640]{2,1,0:T(8,128)(2,1)}), bf16[8,64,640]{2,1,0:T(8,128)(2,1)S(1)}, u32[]{:S(2)}, u32[]{:S(2)}) async-start(bf16[8,64,640]{2,1,0:T(8,128)(2,1)} %all_to_all.130), calls=%async_computation.7 | async-start | bytes 1310720 | tf_op jit(solution)/shard_map/all_to_all | solution.py:59
  273.8 24.0 %all-to-all-start.8 = ((bf16[8,64,640]{2,1,0:T(8,128)(2,1)}), bf16[8,64,640]{2,1,0:T(8,128)(2,1)S(1)}, u32[]{:S(2)}, u32[]{:S(2)}) async-start(bf16[8,64,640]{2,1,0:T(8,128)(2,1)} %all_to_all.134), calls=%async_computation.8 | async-start | bytes 1310720 | tf_op jit(solution)/shard_map/all_to_all | solution.py:60
where the time goes:
time: 300 us; the launch traced here: 299 us
  waiting for transfers between devices  189 us (63%)
  starting transfers between devices  57.5 us (19%)
  local copies, waits for them, and re-layouts  27.6 us (9%)
  matrix products  23.4 us (8%)
    ppermute x4, waiting for transfers between devices, passed_along(): lax.ppermute(value, axis, [(i, (i + by) % devices) for i in range(devices)])  39.7 us
    all_to_all x1, waiting for transfers between devices, per_device(): lax.all_to_all(low_q, 'uly', split_axis=0, concat_axis=1, tiled=True)  29.9 us
    all_to_all x1, waiting for transfers between devices, per_device(): lax.all_to_all(query_rows, 'uly', split_axis=1, concat_axis=0, tiled=True)  20.2 us
    all_to_all x1, waiting for transfers between devices, per_device(): lax.all_to_all(value_rows, 'uly', split_axis=1, concat_axis=0, tiled=True)  20 us
    all_to_all x1, waiting for transfers between devices, per_device(): lax.all_to_all(key_rows, 'uly', split_axis=1, concat_axis=0, tiled=True)  19.6 us
    all_to_all x1, waiting for transfers between devices, per_device(): lax.all_to_all(low_v, 'uly', split_axis=0, concat_axis=1, tiled=True)  17.6 us
    all_to_all x1, waiting for transfers between devices, per_device(): lax.all_to_all(out_grad, 'uly', split_axis=1, concat_axis=0, tiled=True)  16 us
    all_to_all x1, waiting for transfers between devices, per_device(): lax.all_to_all(low_k, 'uly', split_axis=0, concat_axis=1, tiled=True)  14.4 us
  transfers between devices with their start and end apart: 13, of which 11 were waited for; matrix products, arithmetic and copies ran while one was open for 12% of the time, Pallas kernels for 0%

commit v1 on v0

v1 whole, which is shorter than its diff:
```python
import functools

import jax
import jax.numpy as jnp
from jax import lax
from jax.experimental import pallas as pl
from jax.experimental.pallas import tpu as pltpu
from jax.sharding import PartitionSpec as P

F32 = jnp.float32
LOW = jnp.bfloat16
AXES = ("blk", "uly")
CHIPS = 4
RING = 8
NEVER = (RING,) * 8
SWAP_FROM = (2, 6, 2, 6, 2, 6, 2, 6)
PAD = 16


def holder(b, u):
    return b ^ RING if b % RING >= SWAP_FROM[u] else b


def gather_pairs(blocks, d):
    pairs = []
    for b in range(blocks):
        for u in range(2 * CHIPS):
            v = (u + 2 * d) % (2 * CHIPS)
            pairs.append((b * 8 + u, holder(b, v) * 8 + v))
    return pairs


def next_pairs(blocks):
    return [
        (holder(b, u) * 8 + u, holder((b + 1) % blocks, u) * 8 + u)
        for b in range(blocks)
        for u in range(8)
    ]


def back(pairs):
    return [(t, s) for s, t in pairs]


def core_pairs(blocks):
    return [(i, i ^ 1) for i in range(blocks * 8)]


def moved(value, pairs):
    if all(s == t for s, t in pairs):
        return value
    return lax.ppermute(value, AXES, pairs)


def whole(n):
    return [pl.BlockSpec(memory_space=pltpu.VMEM)] * n


def columns(group, width):
    return pl.ds(pl.multiple_of(group * width, 128), width)


def call(kernel, out_shape, place, *arrays, flops=0):
    moved_bytes = sum(a.size * a.dtype.itemsize for a in arrays)
    outs = out_shape if isinstance(out_shape, (list, tuple)) else [out_shape]
    moved_bytes += sum(o.size * o.dtype.itemsize for o in outs)
    return pl.pallas_call(
        kernel,
        out_shape=out_shape,
        in_specs=[pl.BlockSpec(memory_space=pltpu.SMEM)] + whole(len(arrays)),
        out_specs=jax.tree.map(lambda _: pl.BlockSpec(memory_space=pltpu.VMEM), out_shape),
        compiler_params=pltpu.CompilerParams(vmem_limit_bytes=32 << 20),
        cost_estimate=pl.CostEstimate(flops=flops, bytes_accessed=moved_bytes, transcendentals=0),
    )(place, *arrays)


def other_core_parts(first, second, stats, place):
    rows, width = first.shape[0], first.shape[1] // 8
    extra = PAD if stats is not None else 0

    def kernel(place_ref, a_ref, b_ref, *refs):
        out_ref = refs[-1]
        for d in range(CHIPS):
            group = 2 * lax.rem(place_ref[0] + d, CHIPS) + 1 - place_ref[1]
            out_ref[d, :rows] = a_ref[:, columns(group, width)]
            out_ref[d, rows : 2 * rows] = b_ref[:, columns(group, width)]
            if extra:
                out_ref[d, 2 * rows :] = refs[0][group]

    arrays = (first, second) + ((stats,) if extra else ())
    shape = jax.ShapeDtypeStruct((CHIPS, 2 * rows + extra, width), LOW)
    return call(kernel, shape, place, *arrays)


def messages(first, second, stats, other, place):
    rows, width = first.shape[0], first.shape[1] // 8
    extra = PAD if stats is not None else 0

    def kernel(place_ref, a_ref, b_ref, *refs):
        other_ref, outs = refs[-CHIPS - 1], refs[-CHIPS:]
        for d in range(CHIPS):
            group = 2 * lax.rem(place_ref[0] + d, CHIPS) + place_ref[1]
            outs[d][:rows] = a_ref[:, columns(group, width)]
            outs[d][rows : 2 * rows] = b_ref[:, columns(group, width)]
            outs[d][2 * rows : 4 * rows] = other_ref[d, : 2 * rows]
            if extra:
                outs[d][4 * rows :] = jnp.concatenate(
                    [refs[0][group, : PAD // 2], other_ref[d, 2 * rows : 2 * rows + PAD // 2]], axis=0
                )

    arrays = (first, second) + ((stats,) if extra else ()) + (other,)
    shape = [jax.ShapeDtypeStruct((4 * rows + extra, width), LOW)] * CHIPS
    return call(kernel, shape, place, *arrays)


def held(value, *first):
    return pl.pallas_call(
        lambda *refs: None,
        out_shape=jax.ShapeDtypeStruct(value.shape, value.dtype),
        in_specs=[pl.BlockSpec(memory_space=pl.ANY)] * (1 + len(first)),
        out_specs=pl.BlockSpec(memory_space=pl.ANY),
        input_output_aliases={0: 0},
    )(value, *first)


def nt(a, b):
    return lax.dot_general(a, b, (((1,), (1,)), ((), ())), preferred_element_type=F32)


def nn(a, b):
    return lax.dot_general(a, b, (((1,), (0,)), ((), ())), preferred_element_type=F32)


def tn(a, b):
    return lax.dot_general(a, b, (((0,), (0,)), ((), ())), preferred_element_type=F32)


def both(ref, start, rows):
    return [ref[start : start + rows, :], ref[2 * rows + start : 3 * rows + start, :]]


def grads(own, before, keys, heads, rows, scale, so_far=()):
    head = keys[0].shape[1] // heads
    n = len(keys)
    last = len(so_far) > 0

    def kernel(*refs):
        own_refs, before_refs, key_refs = refs[:4], refs[4:8], refs[8 : 8 + n]
        sums_in = refs[8 + n : 8 + n + len(so_far)]
        out_keys, (out_own, out_before) = refs[-2 - n : -2], refs[-2:]
        k = jnp.concatenate(sum((both(r, 0, rows) for r in key_refs), []), axis=0)
        v = jnp.concatenate(sum((both(r, rows, rows) for r in key_refs), []), axis=0)
        grad_k = grad_v = None
        for side, (out_ref, sources) in enumerate(((out_own, own_refs), (out_before, before_refs))):
            for half in range(2):
                pair = sources[2 * half : 2 * half + 2]
                q = jnp.concatenate(sum((both(r, 0, rows) for r in pair), []), axis=0)
                g = jnp.concatenate(sum((both(r, rows, rows) for r in pair), []), axis=0)
                stats = [
                    r[4 * rows + e * (PAD // 2) : 4 * rows + e * (PAD // 2) + 1, :].astype(F32)
                    for r in pair
                    for e in range(2)
                ]
                sums = jnp.concatenate([s[:, :rows] for s in stats], axis=1)
                deltas = jnp.concatenate([s[:, rows:] for s in stats], axis=1)
                prob = jnp.exp(nt(k, q) * scale - sums)
                gv = nn(prob.astype(LOW), g)
                score_grad = (prob * (nt(v, g) - deltas)).astype(LOW)
                gk = nn(score_grad, q)
                grad_k = gk if grad_k is None else grad_k + gk
                grad_v = gv if grad_v is None else grad_v + gv
                gq = tn(score_grad, k) * scale
                at = slice(half * 4 * rows, (half + 1) * 4 * rows)
                if last:
                    gq = gq + sums_in[side][at, :]
                out_ref[at, :] = gq.astype(out_ref.dtype)
        grad_k = (grad_k * scale).astype(LOW)
        grad_v = grad_v.astype(LOW)
        for d in range(n):
            for e in range(2):
                at = (2 * d + e) * rows
                out_keys[d][2 * e * rows : (2 * e + 1) * rows, :] = grad_k[at : at + rows]
                out_keys[d][(2 * e + 1) * rows : (2 * e + 2) * rows, :] = grad_v[at : at + rows]

    width = keys[0].shape[1]
    query_block = pl.BlockSpec((4 * rows + PAD, head), lambda h: (0, h))
    key_block = pl.BlockSpec((4 * rows, head), lambda h: (0, h))
    total = pl.BlockSpec((8 * rows, head), lambda h: (0, h))
    pairs = heads * (2 * n * rows) * (16 * rows)
    out = pl.pallas_call(
        kernel,
        grid=(heads,),
        in_specs=[query_block] * 8 + [key_block] * n + [total] * len(so_far),
        out_specs=[key_block] * n + [total, total],
        out_shape=[jax.ShapeDtypeStruct((4 * rows, width), LOW)] * n
        + [
            jax.ShapeDtypeStruct((8 * rows, width), F32),
            jax.ShapeDtypeStruct((8 * rows, width), LOW if last else F32),
        ],
        compiler_params=pltpu.CompilerParams(
            dimension_semantics=("arbitrary",), vmem_limit_bytes=40 << 20
        ),
        cost_estimate=pl.CostEstimate(
            flops=10 * pairs * head, bytes_accessed=8 << 20, transcendentals=pairs
        ),
    )(*own, *before, *keys, *so_far)
    return out[:n], out[n], out[n + 1]


def query_sums(own, returned, rows):
    def kernel(own_ref, back_ref, *outs):
        for d in range(CHIPS):
            at = slice(2 * d * rows, (2 * d + 2) * rows)
            outs[d][...] = (own_ref[at, :] + back_ref[at, :].astype(F32)).astype(LOW)

    return pl.pallas_call(
        kernel,
        out_shape=[jax.ShapeDtypeStruct((2 * rows, own.shape[1]), LOW)] * CHIPS,
        in_specs=whole(2),
        out_specs=whole(CHIPS),
        compiler_params=pltpu.CompilerParams(vmem_limit_bytes=32 << 20),
    )(own, returned)


def cross_parts(parts, rows):
    shape = jax.ShapeDtypeStruct((CHIPS, parts[0].shape[0] // 2, parts[0].shape[1]), LOW)

    def kernel(*refs):
        half = shape.shape[1]
        for d in range(CHIPS):
            refs[-1][d] = refs[d][half:]

    return pl.pallas_call(
        kernel,
        out_shape=shape,
        in_specs=whole(CHIPS),
        out_specs=whole(1)[0],
        compiler_params=pltpu.CompilerParams(vmem_limit_bytes=32 << 20),
    )(*parts)


def spread(parts, other, place, rows, count):
    width = parts[0].shape[1]

    def kernel(place_ref, *refs):
        other_ref, outs = refs[CHIPS], refs[CHIPS + 1 :]
        for d in range(CHIPS):
            chip = 2 * lax.rem(place_ref[0] + d, CHIPS)
            for i in range(count):
                at = slice(i * rows, (i + 1) * rows)
                outs[i][:, columns(chip + place_ref[1], width)] = refs[d][at]
                outs[i][:, columns(chip + 1 - place_ref[1], width)] = other_ref[d, at]

    shape = [jax.ShapeDtypeStruct((rows, 8 * width), LOW)] * count
    return call(kernel, shape, place, *parts, other)


def per_device(blocks, query_rows, key_rows, value_rows, out_grad, log_sums, deltas):
    rows, heads_total = log_sums.shape
    heads = heads_total // 8
    width = query_rows.shape[1] // 8
    scale = (width // heads) ** (-0.5)
    me = lax.axis_index("uly")
    place = jnp.stack([me // 2, me % 2]).astype(jnp.int32)
    stats = jnp.concatenate([log_sums.T, deltas.T], axis=1).reshape(8, 1, width)
    stats = jnp.pad(stats, ((0, 0), (0, PAD - 1), (0, 0)))

    cores = core_pairs(blocks)
    there = [gather_pairs(blocks, d) for d in range(CHIPS)]
    home = [back(pairs) for pairs in there]
    onward = next_pairs(blocks)

    other = moved(other_core_parts(query_rows, out_grad, stats, place), cores)
    sent = messages(query_rows, out_grad, stats, other, place)
    own = [moved(m, there[d]) for d, m in enumerate(sent)]
    before = [moved(m, onward) for m in own]

    other = moved(other_core_parts(key_rows, value_rows, None, place), cores)
    sent = messages(key_rows, value_rows, None, other, place)
    sent = [
        sent[0],
        held(sent[1], own[1], own[3], *(before[1],)),
        held(sent[2], own[2], *(before[3],)),
        held(sent[3], own[1], own[3], *(before[1],)),
    ]
    keys = [moved(m, there[d]) for d, m in enumerate(sent)]

    first, own_query, cross_query = grads(own, before, (keys[0], keys[1]), heads, rows, scale)
    second, own_query, cross_query = grads(
        own, before, (keys[3], keys[2]), heads, rows, scale, (own_query, cross_query)
    )
    key_grads = (first[0], first[1], second[1], second[0])
    returned = moved(cross_query, back(onward))
    key_home = [moved(m, home[d]) for d, m in enumerate(key_grads)]
    query_grads = query_sums(own_query, returned, rows)
    query_home = [moved(m, home[d]) for d, m in enumerate(query_grads)]

    other = moved(cross_parts(key_home, rows), cores)
    out_k, out_v = spread(key_home, other, place, rows, 2)
    other = moved(cross_parts(query_home, rows), cores)
    (out_q,) = spread(query_home, other, place, rows, 1)
    return out_q, out_k, out_v


def solution(mesh):
    rows = P(AXES, None)
    return jax.shard_map(
        functools.partial(per_device, mesh.shape["blk"]),
        mesh=mesh,
        in_specs=(rows,) * 6,
        out_specs=(rows,) * 3,
        check_vma=False,
    )
```

time: 300 us -> 190 us (0.63)
  the two profiles are of different devices: /device:TPU:6 before, /device:TPU:57 now
where the time goes in v1:
time: 190 us; the launch traced here: 189 us
  starting transfers between devices  100 us (53%)
  waiting for transfers between devices  57.2 us (30%)
  Pallas kernels  22.5 us (12%)
  local copies, waits for them, and re-layouts  7.09 us (4%)
    ppermute x25, starting transfers between devices, moved(): return lax.ppermute(value, AXES, pairs)  100 us
    ppermute x25, waiting for transfers between devices, moved(): return lax.ppermute(value, AXES, pairs)  57.2 us
    pallas_call x2, Pallas kernels, grads(): pl.pallas_call(kernel, grid=(heads,), in_specs=[query_block] * 8 + [key_b...  16.7 us
    unnamed x34, local copies, waits for them, and re-layouts  7.06 us
    pallas_call x6, Pallas kernels, call(): pl.pallas_call(kernel, out_shape=out_shape, in_specs=[pl.BlockSpec(memory...  5.65 us
  transfers between devices with their start and end apart: 25, of which 10 were waited for; matrix products, arithmetic and copies ran while one was open for 0% of the time, Pallas kernels for 6%

profile of v1, /device:TPU:57, one launch (start us, length us, event | category | flops | bytes accessed | tf_op | source)
XLA Modules:
  0.0 189.2 jit_solution(1180887444478552970)
XLA Ops:
  0.6 0.8 pad_maximum_fusion
  1.5 0.1 pad_add_fusion.place_ref
  1.6 0.0 copy-start
  1.6 1.1 copy-done
  2.7 1.1 copy-done.2
  3.8 0.6 shard_map.85
  4.4 0.0 copy-start.1
  4.4 0.0 copy-start.3
  4.4 2.7 %collective-permute-start = (bf16[4,144,640]{2,1,0:T(8,128)(2,1)S(1)}, bf16[4,144,640]{2,1,0:T(8,128)(2,1)S(1)}, u32[]{:S(2)}, u32[]{:S(2)}) collective-permute-start(bf16[4,144,640]{2,1,0:T(8,128)(2,1)S(1)} %shard_map.85), channel_id=1, source_target_pairs={{0,1},{1,0},{2,3},{3,2},{4,5},{5,4},{6,7},{7,6},{8,9},{9,8},{10,11... | collective-permute-start | bytes 2211848 | tf_op jit(solution)/shard_map/ppermute | solution.py:52
  7.1 0.6 shard_map.87
  7.7 1.9 %collective-permute-start.9 = (bf16[4,128,640]{2,1,0:T(8,128)(2,1)S(1)}, bf16[4,128,640]{2,1,0:T(8,128)(2,1)S(1)}, u32[]{:S(2)}, u32[]{:S(2)}) collective-permute-start(bf16[4,128,640]{2,1,0:T(8,128)(2,1)S(1)} %shard_map.87), channel_id=1, source_target_pairs={{0,1},{1,0},{2,3},{3,2},{4,5},{5,4},{6,7},{7,6},{8,9},{9,8},{10,11... | collective-permute-start | bytes 1966088 | tf_op jit(solution)/shard_map/ppermute | solution.py:52
  9.7 0.7 shard_map.86
  10.4 7.6 %collective-permute-start.2 = (bf16[272,640]{1,0:T(8,128)(2,1)S(1)}, bf16[272,640]{1,0:T(8,128)(2,1)S(1)}, u32[]{:S(2)}, u32[]{:S(2)}) collective-permute-start(bf16[272,640]{1,0:T(8,128)(2,1)S(1)} %get-tuple-element.26), channel_id=1, source_target_pairs={{0,2},{1,3},{2,4},{3,5},{4,6},{5,7},{6,0},{7,1},{8,10},{9,11},{10,... | collective-permute-start | bytes 1044488 | tf_op jit(solution)/shard_map/ppermute | solution.py:52
  18.0 5.0 %collective-permute-start.4 = (bf16[272,640]{1,0:T(8,128)(2,1)S(1)}, bf16[272,640]{1,0:T(8,128)(2,1)}, u32[]{:S(2)}, u32[]{:S(2)}) collective-permute-start(bf16[272,640]{1,0:T(8,128)(2,1)S(1)} %get-tuple-element.28), channel_id=1, source_target_pairs={{0,6},{1,7},{2,0},{3,1},{4,2},{5,3},{6,4},{7,5},{8,14},{9,15},{10,... | collective-permute-start | bytes 1044488 | tf_op jit(solution)/shard_map/ppermute | solution.py:52
  23.0 3.1 %collective-permute-start.1 = (bf16[272,640]{1,0:T(8,128)(2,1)S(1)}, bf16[272,640]{1,0:T(8,128)(2,1)S(1)}, u32[]{:S(2)}, u32[]{:S(2)}) collective-permute-start(bf16[272,640]{1,0:T(8,128)(2,1)S(1)} %get-tuple-element.25), channel_id=1, source_target_pairs={{0,0},{1,1},{2,2},{3,3},{4,4},{5,5},{6,6},{7,7},{8,8},{9,9},{10,10... | collective-permute-start | bytes 1044488 | tf_op jit(solution)/shard_map/ppermute | solution.py:52
  26.1 5.2 %collective-permute-start.3 = (bf16[272,640]{1,0:T(8,128)(2,1)S(1)}, bf16[272,640]{1,0:T(8,128)(2,1)S(1)}, u32[]{:S(2)}, u32[]{:S(2)}) collective-permute-start(bf16[272,640]{1,0:T(8,128)(2,1)S(1)} %get-tuple-element.27), channel_id=1, source_target_pairs={{0,4},{1,5},{2,6},{3,7},{4,0},{5,1},{6,2},{7,3},{8,12},{9,13},{10,... | collective-permute-start | bytes 1044488 | tf_op jit(solution)/shard_map/ppermute | solution.py:52
  31.3 7.0 %collective-permute-done.2.refs_1_ = bf16[272,640]{1,0:T(8,128)(2,1)S(1)} collective-permute-done((bf16[272,640]{1,0:T(8,128)(2,1)S(1)}, bf16[272,640]{1,0:T(8,128)(2,1)S(1)}, u32[]{:S(2)}, u32[]{:S(2)}) %collective-permute-start.2) | collective-permute-done | bytes 348192 | tf_op jit(solution)/shard_map/ppermute | solution.py:52
  38.2 1.9 %collective-permute-start.6 = (bf16[272,640]{1,0:T(8,128)(2,1)S(1)}, bf16[272,640]{1,0:T(8,128)(2,1)S(1)}, u32[]{:S(2)}, u32[]{:S(2)}) collective-permute-start(bf16[272,640]{1,0:T(8,128)(2,1)S(1)} %collective-permute-done.2.refs_1_), channel_id=1, source_target_pairs={{0,8},{1,9},{2,10},{3,11},{4,12},{5,13},{6,14},{7,15},{8,80},{9,17... | collective-permute-start | bytes 1044488 | tf_op jit(solution)/shard_map/ppermute | solution.py:52
  40.2 1.9 %collective-permute-start.8 = (bf16[272,640]{1,0:T(8,128)(2,1)}, bf16[272,640]{1,0:T(8,128)(2,1)S(1)}, u32[]{:S(2)}, u32[]{:S(2)}) collective-permute-start(bf16[272,640]{1,0:T(8,128)(2,1)} %collective-permute-done.4.refs_2_.refs_3_), channel_id=1, source_target_pairs={{0,8},{1,9},{2,10},{3,11},{4,12},{5,13},{6,14},{7,15},{8,80},{9,17... | collective-permute-start | bytes 1044488 | tf_op jit(solution)/shard_map/ppermute | solution.py:52
  42.1 0.6 shard_map.88
  42.8 0.7 copy-done.14
  43.5 0.7 copy-done.15
  44.2 0.7 copy-done.16
  44.9 4.5 %collective-permute-start.12 = (bf16[256,640]{1,0:T(8,128)(2,1)S(1)}, bf16[256,640]{1,0:T(8,128)(2,1)S(1)}, u32[]{:S(2)}, u32[]{:S(2)}) collective-permute-start(bf16[256,640]{1,0:T(8,128)(2,1)S(1)} %get-tuple-element.31), channel_id=1, source_target_pairs={{0,0},{1,1},{2,2},{3,3},{4,4},{5,5},{6,6},{7,7},{8,8},{9,9},{10,10... | collective-permute-start | bytes 983048 | tf_op jit(solution)/shard_map/ppermute | solution.py:52
  49.4 4.8 %collective-permute-done.1.refs_0_ = bf16[272,640]{1,0:T(8,128)(2,1)S(1)} collective-permute-done((bf16[272,640]{1,0:T(8,128)(2,1)S(1)}, bf16[272,640]{1,0:T(8,128)(2,1)S(1)}, u32[]{:S(2)}, u32[]{:S(2)}) %collective-permute-start.1) | collective-permute-done | bytes 348192 | tf_op jit(solution)/shard_map/ppermute | solution.py:52
  54.2 1.9 %collective-permute-start.5 = (bf16[272,640]{1,0:T(8,128)(2,1)S(1)}, bf16[272,640]{1,0:T(8,128)(2,1)S(1)}, u32[]{:S(2)}, u32[]{:S(2)}) collective-permute-start(bf16[272,640]{1,0:T(8,128)(2,1)S(1)} %collective-permute-done.1.refs_0_), channel_id=1, source_target_pairs={{0,8},{1,9},{2,10},{3,11},{4,12},{5,13},{6,14},{7,15},{8,80},{9,17... | collective-permute-start | bytes 1044488 | tf_op jit(solution)/shard_map/ppermute | solution.py:52
  56.1 0.0 copy-start.10
  56.1 1.9 %collective-permute-start.7 = (bf16[272,640]{1,0:T(8,128)(2,1)S(1)}, bf16[272,640]{1,0:T(8,128)(2,1)S(1)}, u32[]{:S(2)}, u32[]{:S(2)}) collective-permute-start(bf16[272,640]{1,0:T(8,128)(2,1)S(1)} %collective-permute-done.3.refs_1_.refs_2_), channel_id=1, source_target_pairs={{0,8},{1,9},{2,10},{3,11},{4,12},{5,13},{6,14},{7,15},{8,80},{9,17... | collective-permute-start | bytes 1044488 | tf_op jit(solution)/shard_map/ppermute | solution.py:52
  58.1 0.0 collective-permute-done.6.refs_3_.refs_5_
  58.1 0.0 copy-start.8
  58.1 0.7 copy-done.8
  58.8 5.5 %collective-permute-start.13 = (bf16[256,640]{1,0:T(8,128)(2,1)}, bf16[256,640]{1,0:T(8,128)(2,1)}, u32[]{:S(2)}, u32[]{:S(2)}) collective-permute-start(bf16[256,640]{1,0:T(8,128)(2,1)} %shard_map.91), channel_id=1, source_target_pairs={{0,2},{1,3},{2,4},{3,5},{4,6},{5,7},{6,0},{7,1},{8,10},{9,11},{10,... | collective-permute-start | bytes 983048 | tf_op jit(solution)/shard_map/ppermute | solution.py:52
  64.3 0.0 copy-start.7
  64.3 0.0 copy-start.9
  64.3 3.8 %collective-permute-start.10 = (bf16[256,640]{1,0:T(8,128)(2,1)}, bf16[256,640]{1,0:T(8,128)(2,1)S(1)}, u32[]{:S(2)}, u32[]{:S(2)}) collective-permute-start(bf16[256,640]{1,0:T(8,128)(2,1)} %shard_map.89), channel_id=1, source_target_pairs={{0,6},{1,7},{2,0},{3,1},{4,2},{5,3},{6,4},{7,5},{8,14},{9,15},{10,... | collective-permute-start | bytes 983048 | tf_op jit(solution)/shard_map/ppermute | solution.py:52
  68.2 6.8 %collective-permute-start.11 = (bf16[256,640]{1,0:T(8,128)(2,1)}, bf16[256,640]{1,0:T(8,128)(2,1)S(1)}, u32[]{:S(2)}, u32[]{:S(2)}) collective-permute-start(bf16[256,640]{1,0:T(8,128)(2,1)} %shard_map.90), channel_id=1, source_target_pairs={{0,4},{1,5},{2,6},{3,7},{4,0},{5,1},{6,2},{7,3},{8,12},{9,13},{10,... | collective-permute-start | bytes 983048 | tf_op jit(solution)/shard_map/ppermute | solution.py:52
  75.0 5.0 %collective-permute-done.7.refs_6_ = bf16[272,640]{1,0:T(8,128)(2,1)S(1)} collective-permute-done((bf16[272,640]{1,0:T(8,128)(2,1)S(1)}, bf16[272,640]{1,0:T(8,128)(2,1)S(1)}, u32[]{:S(2)}, u32[]{:S(2)}) %collective-permute-start.7) | collective-permute-done | bytes 348192 | tf_op jit(solution)/shard_map/ppermute | solution.py:52
  80.1 0.0 copy-start.11
  80.1 1.0 copy-done.11
  81.1 1.0 copy-done.13
  82.0 8.3 %shard_map.92 = (bf16[256,640]{1,0:T(8,128)(2,1)S(1)}, bf16[256,640]{1,0:T(8,128)(2,1)S(1)}, f32[512,640]{1,0:T(8,128)S(1)}, f32[512,640]{1,0:T(8,128)S(1)}) custom-call(bf16[272,640]{1,0:T(8,128)(2,1)S(1)} %collective-permute-done.1.refs_0_, bf16[272,640]{1,0:T(8,128)(2,1)S(1)} %copy-done.7, bf16[272,640]{1,0:T(8,128)(2,1)S(1)} %copy-done.11, ...), custom_call_target="tpu_custom_call" | custom-call | flops 1677721600 | bytes 8388608 | tf_op jit(solution)/shard_map/pallas_call | solution.py:190
  90.3 0.6 collective-permute-done.11.refs_9_
  90.9 8.4 %shard_map.93 = (bf16[256,640]{1,0:T(8,128)(2,1)S(1)}, bf16[256,640]{1,0:T(8,128)(2,1)S(1)}, f32[512,640]{1,0:T(8,128)S(1)}, bf16[512,640]{1,0:T(8,128)(2,1)S(1)}) custom-call(bf16[272,640]{1,0:T(8,128)(2,1)S(1)} %collective-permute-done.1.refs_0_, bf16[272,640]{1,0:T(8,128)(2,1)S(1)} %copy-done.7, bf16[272,640]{1,0:T(8,128)(2,1)S(1)} %copy-done.11, ...), custom_call_target="tpu_custom_call" | custom-call | flops 1677721600 | bytes 8388608 | tf_op jit(solution)/shard_map/pallas_call | solution.py:190
  99.4 10.4 %collective-permute-start.14 = (bf16[512,640]{1,0:T(8,128)(2,1)S(1)}, bf16[512,640]{1,0:T(8,128)(2,1)S(1)}, u32[]{:S(2)}, u32[]{:S(2)}) collective-permute-start(bf16[512,640]{1,0:T(8,128)(2,1)S(1)} %get-tuple-element.36), channel_id=1, source_target_pairs={{8,0},{9,1},{10,2},{11,3},{12,4},{13,5},{14,6},{15,7},{80,8},{17,9... | collective-permute-start | bytes 1966088 | tf_op jit(solution)/shard_map/ppermute | solution.py:52
  109.7 8.4 %collective-permute-start.22 = (bf16[256,640]{1,0:T(8,128)(2,1)S(1)}, bf16[256,640]{1,0:T(8,128)(2,1)S(1)}, u32[]{:S(2)}, u32[]{:S(2)}) collective-permute-start(bf16[256,640]{1,0:T(8,128)(2,1)S(1)} %get-tuple-element.43), channel_id=1, source_target_pairs={{4,0},{5,1},{6,2},{7,3},{0,4},{1,5},{2,6},{3,7},{12,8},{13,9},{14,... | collective-permute-start | bytes 983048 | tf_op jit(solution)/shard_map/ppermute | solution.py:52
  118.2 2.8 %collective-permute-start.23 = (bf16[256,640]{1,0:T(8,128)(2,1)S(1)}, bf16[256,640]{1,0:T(8,128)(2,1)S(1)}, u32[]{:S(2)}, u32[]{:S(2)}) collective-permute-start(bf16[256,640]{1,0:T(8,128)(2,1)S(1)} %get-tuple-element.44), channel_id=1, source_target_pairs={{6,0},{7,1},{0,2},{1,3},{2,4},{3,5},{4,6},{5,7},{14,8},{15,9},{8,1... | collective-permute-start | bytes 983048 | tf_op jit(solution)/shard_map/ppermute | solution.py:52
  120.9 1.9 %collective-permute-start.20 = (bf16[256,640]{1,0:T(8,128)(2,1)S(1)}, bf16[256,640]{1,0:T(8,128)(2,1)S(1)}, u32[]{:S(2)}, u32[]{:S(2)}) collective-permute-start(bf16[256,640]{1,0:T(8,128)(2,1)S(1)} %get-tuple-element.41), channel_id=1, source_target_pairs={{0,0},{1,1},{2,2},{3,3},{4,4},{5,5},{6,6},{7,7},{8,8},{9,9},{10,10... | collective-permute-start | bytes 983048 | tf_op jit(solution)/shard_map/ppermute | solution.py:52
  122.9 5.2 %collective-permute-start.21 = (bf16[256,640]{1,0:T(8,128)(2,1)S(1)}, bf16[256,640]{1,0:T(8,128)(2,1)S(1)}, u32[]{:S(2)}, u32[]{:S(2)}) collective-permute-start(bf16[256,640]{1,0:T(8,128)(2,1)S(1)} %get-tuple-element.42), channel_id=1, source_target_pairs={{2,0},{3,1},{4,2},{5,3},{6,4},{7,5},{0,6},{1,7},{10,8},{11,9},{12,... | collective-permute-start | bytes 983048 | tf_op jit(solution)/shard_map/ppermute | solution.py:52
  128.1 5.1 %collective-permute-done.22.refs_2_ = bf16[256,640]{1,0:T(8,128)(2,1)S(1)} collective-permute-done((bf16[256,640]{1,0:T(8,128)(2,1)S(1)}, bf16[256,640]{1,0:T(8,128)(2,1)S(1)}, u32[]{:S(2)}, u32[]{:S(2)}) %collective-permute-start.22) | collective-permute-done | bytes 327712 | tf_op jit(solution)/shard_map/ppermute | solution.py:52
  133.2 12.1 %collective-permute-done.23.refs_3_ = bf16[256,640]{1,0:T(8,128)(2,1)S(1)} collective-permute-done((bf16[256,640]{1,0:T(8,128)(2,1)S(1)}, bf16[256,640]{1,0:T(8,128)(2,1)S(1)}, u32[]{:S(2)}, u32[]{:S(2)}) %collective-permute-start.23) | collective-permute-done | bytes 327712 | tf_op jit(solution)/shard_map/ppermute | solution.py:52
  145.2 1.7 collective-permute-done.20.refs_0_
  146.9 8.6 %collective-permute-done.21.refs_1_ = bf16[256,640]{1,0:T(8,128)(2,1)S(1)} collective-permute-done((bf16[256,640]{1,0:T(8,128)(2,1)S(1)}, bf16[256,640]{1,0:T(8,128)(2,1)S(1)}, u32[]{:S(2)}, u32[]{:S(2)}) %collective-permute-start.21) | collective-permute-done | bytes 327712 | tf_op jit(solution)/shard_map/ppermute | solution.py:52
  155.5 0.1 shard_map.97
  155.5 2.4 %collective-permute-start.24 = (bf16[4,128,640]{2,1,0:T(8,128)(2,1)S(1)}, bf16[4,128,640]{2,1,0:T(8,128)(2,1)S(1)}, u32[]{:S(2)}, u32[]{:S(2)}) collective-permute-start(bf16[4,128,640]{2,1,0:T(8,128)(2,1)S(1)} %shard_map.97), channel_id=1, source_target_pairs={{0,1},{1,0},{2,3},{3,2},{4,5},{5,4},{6,7},{7,6},{8,9},{9,8},{10,11... | collective-permute-start | bytes 1966088 | tf_op jit(solution)/shard_map/ppermute | solution.py:52
  158.0 0.1 shard_map.94
  158.1 1.9 %collective-permute-start.15 = (bf16[128,640]{1,0:T(8,128)(2,1)S(1)}, bf16[128,640]{1,0:T(8,128)(2,1)S(1)}, u32[]{:S(2)}, u32[]{:S(2)}) collective-permute-start(bf16[128,640]{1,0:T(8,128)(2,1)S(1)} %get-tuple-element.37), channel_id=1, source_target_pairs={{0,0},{1,1},{2,2},{3,3},{4,4},{5,5},{6,6},{7,7},{8,8},{9,9},{10,10... | collective-permute-start | bytes 491528 | tf_op jit(solution)/shard_map/ppermute | solution.py:52
  160.0 1.9 %collective-permute-start.16 = (bf16[128,640]{1,0:T(8,128)(2,1)S(1)}, bf16[128,640]{1,0:T(8,128)(2,1)S(1)}, u32[]{:S(2)}, u32[]{:S(2)}) collective-permute-start(bf16[128,640]{1,0:T(8,128)(2,1)S(1)} %get-tuple-element.38), channel_id=1, source_target_pairs={{2,0},{3,1},{4,2},{5,3},{6,4},{7,5},{0,6},{1,7},{10,8},{11,9},{12,... | collective-permute-start | bytes 491528 | tf_op jit(solution)/shard_map/ppermute | solution.py:52
  162.0 4.9 %collective-permute-start.17 = (bf16[128,640]{1,0:T(8,128)(2,1)S(1)}, bf16[128,640]{1,0:T(8,128)(2,1)S(1)}, u32[]{:S(2)}, u32[]{:S(2)}) collective-permute-start(bf16[128,640]{1,0:T(8,128)(2,1)S(1)} %get-tuple-element.39), channel_id=1, source_target_pairs={{4,0},{5,1},{6,2},{7,3},{0,4},{1,5},{2,6},{3,7},{12,8},{13,9},{14,... | collective-permute-start | bytes 491528 | tf_op jit(solution)/shard_map/ppermute | solution.py:52
  166.9 4.3 %collective-permute-start.18 = (bf16[128,640]{1,0:T(8,128)(2,1)S(1)}, bf16[128,640]{1,0:T(8,128)(2,1)S(1)}, u32[]{:S(2)}, u32[]{:S(2)}) collective-permute-start(bf16[128,640]{1,0:T(8,128)(2,1)S(1)} %get-tuple-element.40), channel_id=1, source_target_pairs={{6,0},{7,1},{0,2},{1,3},{2,4},{3,5},{4,6},{5,7},{14,8},{15,9},{8,1... | collective-permute-start | bytes 491528 | tf_op jit(solution)/shard_map/ppermute | solution.py:52
  171.2 2.3 %collective-permute-done.17.refs_2_ = bf16[128,640]{1,0:T(8,128)(2,1)S(1)} collective-permute-done((bf16[128,640]{1,0:T(8,128)(2,1)S(1)}, bf16[128,640]{1,0:T(8,128)(2,1)S(1)}, u32[]{:S(2)}, u32[]{:S(2)}) %collective-permute-start.17) | collective-permute-done | bytes 163872 | tf_op jit(solution)/shard_map/ppermute | solution.py:52
  173.4 10.1 %collective-permute-done.18.refs_3_ = bf16[128,640]{1,0:T(8,128)(2,1)S(1)} collective-permute-done((bf16[128,640]{1,0:T(8,128)(2,1)S(1)}, bf16[128,640]{1,0:T(8,128)(2,1)S(1)}, u32[]{:S(2)}, u32[]{:S(2)}) %collective-permute-start.18) | collective-permute-done | bytes 163872 | tf_op jit(solution)/shard_map/ppermute | solution.py:52
  183.6 2.4 %collective-permute-start.19 = (bf16[4,64,640]{2,1,0:T(8,128)(2,1)S(1)}, bf16[4,64,640]{2,1,0:T(8,128)(2,1)S(1)}, u32[]{:S(2)}, u32[]{:S(2)}) collective-permute-start(bf16[4,64,640]{2,1,0:T(8,128)(2,1)S(1)} %shard_map.95), channel_id=1, source_target_pairs={{0,1},{1,0},{2,3},{3,2},{4,5},{5,4},{6,7},{7,6},{8,9},{9,8},{10,11... | collective-permute-start | bytes 983048 | tf_op jit(solution)/shard_map/ppermute | solution.py:52
  186.0 1.7 shard_map.98
  187.7 1.4 shard_map.96
  (38 shorter events, 0.1 us)
Async XLA Ops:
  1.6 1.1 copy-start
  2.7 1.1 copy-start.2
  3.8 3.4 %copy-start.4 = (bf16[64,5120]{1,0:T(8,128)(2,1)S(1)}, bf16[64,5120]{1,0:T(8,128)(2,1)}, u32[]{:S(2)}) copy-start(bf16[64,5120]{1,0:T(8,128)(2,1)} %a_ref.7) | copy-start | bytes 1966084
  3.8 3.4 %copy-start.5 = (bf16[64,5120]{1,0:T(8,128)(2,1)S(1)}, bf16[64,5120]{1,0:T(8,128)(2,1)}, u32[]{:S(2)}) copy-start(bf16[64,5120]{1,0:T(8,128)(2,1)} %b_ref.7) | copy-start | bytes 1966084
  4.4 5.3 %copy-start.1 = (bf16[64,5120]{1,0:T(8,128)(2,1)S(1)}, bf16[64,5120]{1,0:T(8,128)(2,1)}, u32[]{:S(2)}) copy-start(bf16[64,5120]{1,0:T(8,128)(2,1)} %a_ref.5) | copy-start | bytes 1966084
  4.4 5.3 %copy-start.3 = (bf16[64,5120]{1,0:T(8,128)(2,1)S(1)}, bf16[64,5120]{1,0:T(8,128)(2,1)}, u32[]{:S(2)}) copy-start(bf16[64,5120]{1,0:T(8,128)(2,1)} %b_ref.5) | copy-start | bytes 1966084
  4.4 5.3 %collective-permute-start = (bf16[4,144,640]{2,1,0:T(8,128)(2,1)S(1)}, bf16[4,144,640]{2,1,0:T(8,128)(2,1)S(1)}, u32[]{:S(2)}, u32[]{:S(2)}) collective-permute-start(bf16[4,144,640]{2,1,0:T(8,128)(2,1)S(1)} %shard_map.85), channel_id=1, source_target_pairs={{0,1},{1,0},{2,3},{3,2},{4,5},{5,4},{6,7},{7,6},{8,9},{9,8},{10,11... | collective-permute-start | bytes 2211848 | tf_op jit(solution)/shard_map/ppermute | solution.py:52
  7.7 34.3 %collective-permute-start.9 = (bf16[4,128,640]{2,1,0:T(8,128)(2,1)S(1)}, bf16[4,128,640]{2,1,0:T(8,128)(2,1)S(1)}, u32[]{:S(2)}, u32[]{:S(2)}) collective-permute-start(bf16[4,128,640]{2,1,0:T(8,128)(2,1)S(1)} %shard_map.87), channel_id=1, source_target_pairs={{0,1},{1,0},{2,3},{3,2},{4,5},{5,4},{6,7},{7,6},{8,9},{9,8},{10,11... | collective-permute-start | bytes 1966088 | tf_op jit(solution)/shard_map/ppermute | solution.py:52
  10.4 27.9 %collective-permute-start.2 = (bf16[272,640]{1,0:T(8,128)(2,1)S(1)}, bf16[272,640]{1,0:T(8,128)(2,1)S(1)}, u32[]{:S(2)}, u32[]{:S(2)}) collective-permute-start(bf16[272,640]{1,0:T(8,128)(2,1)S(1)} %get-tuple-element.26), channel_id=1, source_target_pairs={{0,2},{1,3},{2,4},{3,5},{4,6},{5,7},{6,0},{7,1},{8,10},{9,11},{10,... | collective-permute-start | bytes 1044488 | tf_op jit(solution)/shard_map/ppermute | solution.py:52
  18.0 22.2 %collective-permute-start.4 = (bf16[272,640]{1,0:T(8,128)(2,1)S(1)}, bf16[272,640]{1,0:T(8,128)(2,1)}, u32[]{:S(2)}, u32[]{:S(2)}) collective-permute-start(bf16[272,640]{1,0:T(8,128)(2,1)S(1)} %get-tuple-element.28), channel_id=1, source_target_pairs={{0,6},{1,7},{2,0},{3,1},{4,2},{5,3},{6,4},{7,5},{8,14},{9,15},{10,... | collective-permute-start | bytes 1044488 | tf_op jit(solution)/shard_map/ppermute | solution.py:52
  23.0 31.2 %collective-permute-start.1 = (bf16[272,640]{1,0:T(8,128)(2,1)S(1)}, bf16[272,640]{1,0:T(8,128)(2,1)S(1)}, u32[]{:S(2)}, u32[]{:S(2)}) collective-permute-start(bf16[272,640]{1,0:T(8,128)(2,1)S(1)} %get-tuple-element.25), channel_id=1, source_target_pairs={{0,0},{1,1},{2,2},{3,3},{4,4},{5,5},{6,6},{7,7},{8,8},{9,9},{10,10... | collective-permute-start | bytes 1044488 | tf_op jit(solution)/shard_map/ppermute | solution.py:52
  26.1 30.1 %collective-permute-start.3 = (bf16[272,640]{1,0:T(8,128)(2,1)S(1)}, bf16[272,640]{1,0:T(8,128)(2,1)S(1)}, u32[]{:S(2)}, u32[]{:S(2)}) collective-permute-start(bf16[272,640]{1,0:T(8,128)(2,1)S(1)} %get-tuple-element.27), channel_id=1, source_target_pairs={{0,4},{1,5},{2,6},{3,7},{4,0},{5,1},{6,2},{7,3},{8,12},{9,13},{10,... | collective-permute-start | bytes 1044488 | tf_op jit(solution)/shard_map/ppermute | solution.py:52
  38.2 19.9 %copy-start.6 = (bf16[272,640]{1,0:T(8,128)(2,1)}, bf16[272,640]{1,0:T(8,128)(2,1)S(1)}, u32[]{:S(2)}) copy-start(bf16[272,640]{1,0:T(8,128)(2,1)S(1)} %collective-permute-done.2.refs_1_) | copy-start | bytes 1044484
  38.2 19.8 %collective-permute-start.6 = (bf16[272,640]{1,0:T(8,128)(2,1)S(1)}, bf16[272,640]{1,0:T(8,128)(2,1)S(1)}, u32[]{:S(2)}, u32[]{:S(2)}) collective-permute-start(bf16[272,640]{1,0:T(8,128)(2,1)S(1)} %collective-permute-done.2.refs_1_), channel_id=1, source_target_pairs={{0,8},{1,9},{2,10},{3,11},{4,12},{5,13},{6,14},{7,15},{8,80},{9,17... | collective-permute-start | bytes 1044488 | tf_op jit(solution)/shard_map/ppermute | solution.py:52
  40.2 24.2 %collective-permute-start.8 = (bf16[272,640]{1,0:T(8,128)(2,1)}, bf16[272,640]{1,0:T(8,128)(2,1)S(1)}, u32[]{:S(2)}, u32[]{:S(2)}) collective-permute-start(bf16[272,640]{1,0:T(8,128)(2,1)} %collective-permute-done.4.refs_2_.refs_3_), channel_id=1, source_target_pairs={{0,8},{1,9},{2,10},{3,11},{4,12},{5,13},{6,14},{7,15},{8,80},{9,17... | collective-permute-start | bytes 1044488 | tf_op jit(solution)/shard_map/ppermute | solution.py:52
  42.7 0.7 copy-start.14
  43.5 0.7 copy-start.15
  44.2 0.7 copy-start.16
  44.9 23.3 %collective-permute-start.12 = (bf16[256,640]{1,0:T(8,128)(2,1)S(1)}, bf16[256,640]{1,0:T(8,128)(2,1)S(1)}, u32[]{:S(2)}, u32[]{:S(2)}) collective-permute-start(bf16[256,640]{1,0:T(8,128)(2,1)S(1)} %get-tuple-element.31), channel_id=1, source_target_pairs={{0,0},{1,1},{2,2},{3,3},{4,4},{5,5},{6,6},{7,7},{8,8},{9,9},{10,10... | collective-permute-start | bytes 983048 | tf_op jit(solution)/shard_map/ppermute | solution.py:52
  54.2 20.8 %collective-permute-start.5 = (bf16[272,640]{1,0:T(8,128)(2,1)S(1)}, bf16[272,640]{1,0:T(8,128)(2,1)S(1)}, u32[]{:S(2)}, u32[]{:S(2)}) collective-permute-start(bf16[272,640]{1,0:T(8,128)(2,1)S(1)} %collective-permute-done.1.refs_0_), channel_id=1, source_target_pairs={{0,8},{1,9},{2,10},{3,11},{4,12},{5,13},{6,14},{7,15},{8,80},{9,17... | collective-permute-start | bytes 1044488 | tf_op jit(solution)/shard_map/ppermute | solution.py:52
  56.1 12.1 %copy-start.10 = (bf16[272,640]{1,0:T(8,128)(2,1)}, bf16[272,640]{1,0:T(8,128)(2,1)S(1)}, u32[]{:S(2)}) copy-start(bf16[272,640]{1,0:T(8,128)(2,1)S(1)} %collective-permute-done.3.refs_1_.refs_2_) | copy-start | bytes 1044484
  56.1 23.9 %collective-permute-start.7 = (bf16[272,640]{1,0:T(8,128)(2,1)S(1)}, bf16[272,640]{1,0:T(8,128)(2,1)S(1)}, u32[]{:S(2)}, u32[]{:S(2)}) collective-permute-start(bf16[272,640]{1,0:T(8,128)(2,1)S(1)} %collective-permute-done.3.refs_1_.refs_2_), channel_id=1, source_target_pairs={{0,8},{1,9},{2,10},{3,11},{4,12},{5,13},{6,14},{7,15},{8,80},{9,17... | collective-permute-start | bytes 1044488 | tf_op jit(solution)/shard_map/ppermute | solution.py:52
  58.1 0.7 copy-start.8
  58.8 21.3 %collective-permute-start.13 = (bf16[256,640]{1,0:T(8,128)(2,1)}, bf16[256,640]{1,0:T(8,128)(2,1)}, u32[]{:S(2)}, u32[]{:S(2)}) collective-permute-start(bf16[256,640]{1,0:T(8,128)(2,1)} %shard_map.91), channel_id=1, source_target_pairs={{0,2},{1,3},{2,4},{3,5},{4,6},{5,7},{6,0},{7,1},{8,10},{9,11},{10,... | collective-permute-start | bytes 983048 | tf_op jit(solution)/shard_map/ppermute | solution.py:52
  64.3 15.8 %copy-start.7 = (bf16[272,640]{1,0:T(8,128)(2,1)S(1)}, bf16[272,640]{1,0:T(8,128)(2,1)}, u32[]{:S(2)}) copy-start(bf16[272,640]{1,0:T(8,128)(2,1)} %copy-done.6) | copy-start | bytes 1044484
  64.3 15.8 %copy-start.9 = (bf16[272,640]{1,0:T(8,128)(2,1)S(1)}, bf16[272,640]{1,0:T(8,128)(2,1)}, u32[]{:S(2)}) copy-start(bf16[272,640]{1,0:T(8,128)(2,1)} %copy-done.8) | copy-start | bytes 1044484
  64.3 3.9 %copy-start.12 = (bf16[272,640]{1,0:T(8,128)(2,1)}, bf16[272,640]{1,0:T(8,128)(2,1)S(1)}, u32[]{:S(2)}) copy-start(bf16[272,640]{1,0:T(8,128)(2,1)S(1)} %collective-permute-done.8.refs_2_.refs_7_) | copy-start | bytes 1044484
  64.3 26.0 %collective-permute-start.10 = (bf16[256,640]{1,0:T(8,128)(2,1)}, bf16[256,640]{1,0:T(8,128)(2,1)S(1)}, u32[]{:S(2)}, u32[]{:S(2)}) collective-permute-start(bf16[256,640]{1,0:T(8,128)(2,1)} %shard_map.89), channel_id=1, source_target_pairs={{0,6},{1,7},{2,0},{3,1},{4,2},{5,3},{6,4},{7,5},{8,14},{9,15},{10,... | collective-permute-start | bytes 983048 | tf_op jit(solution)/shard_map/ppermute | solution.py:52
  68.2 22.7 %collective-permute-start.11 = (bf16[256,640]{1,0:T(8,128)(2,1)}, bf16[256,640]{1,0:T(8,128)(2,1)S(1)}, u32[]{:S(2)}, u32[]{:S(2)}) collective-permute-start(bf16[256,640]{1,0:T(8,128)(2,1)} %shard_map.90), channel_id=1, source_target_pairs={{0,4},{1,5},{2,6},{3,7},{4,0},{5,1},{6,2},{7,3},{8,12},{9,13},{10,... | collective-permute-start | bytes 983048 | tf_op jit(solution)/shard_map/ppermute | solution.py:52
  80.1 1.0 copy-start.11
  81.1 1.0 copy-start.13
  99.4 58.6 %collective-permute-start.14 = (bf16[512,640]{1,0:T(8,128)(2,1)S(1)}, bf16[512,640]{1,0:T(8,128)(2,1)S(1)}, u32[]{:S(2)}, u32[]{:S(2)}) collective-permute-start(bf16[512,640]{1,0:T(8,128)(2,1)S(1)} %get-tuple-element.36), channel_id=1, source_target_pairs={{8,0},{9,1},{10,2},{11,3},{12,4},{13,5},{14,6},{15,7},{80,8},{17,9... | collective-permute-start | bytes 1966088 | tf_op jit(solution)/shard_map/ppermute | solution.py:52
  109.7 23.4 %collective-permute-start.22 = (bf16[256,640]{1,0:T(8,128)(2,1)S(1)}, bf16[256,640]{1,0:T(8,128)(2,1)S(1)}, u32[]{:S(2)}, u32[]{:S(2)}) collective-permute-start(bf16[256,640]{1,0:T(8,128)(2,1)S(1)} %get-tuple-element.43), channel_id=1, source_target_pairs={{4,0},{5,1},{6,2},{7,3},{0,4},{1,5},{2,6},{3,7},{12,8},{13,9},{14,... | collective-permute-start | bytes 983048 | tf_op jit(solution)/shard_map/ppermute | solution.py:52
  118.2 27.1 %collective-permute-start.23 = (bf16[256,640]{1,0:T(8,128)(2,1)S(1)}, bf16[256,640]{1,0:T(8,128)(2,1)S(1)}, u32[]{:S(2)}, u32[]{:S(2)}) collective-permute-start(bf16[256,640]{1,0:T(8,128)(2,1)S(1)} %get-tuple-element.44), channel_id=1, source_target_pairs={{6,0},{7,1},{0,2},{1,3},{2,4},{3,5},{4,6},{5,7},{14,8},{15,9},{8,1... | collective-permute-start | bytes 983048 | tf_op jit(solution)/shard_map/ppermute | solution.py:52
  120.9 26.0 %collective-permute-start.20 = (bf16[256,640]{1,0:T(8,128)(2,1)S(1)}, bf16[256,640]{1,0:T(8,128)(2,1)S(1)}, u32[]{:S(2)}, u32[]{:S(2)}) collective-permute-start(bf16[256,640]{1,0:T(8,128)(2,1)S(1)} %get-tuple-element.41), channel_id=1, source_target_pairs={{0,0},{1,1},{2,2},{3,3},{4,4},{5,5},{6,6},{7,7},{8,8},{9,9},{10,10... | collective-permute-start | bytes 983048 | tf_op jit(solution)/shard_map/ppermute | solution.py:52
  122.9 32.6 %collective-permute-start.21 = (bf16[256,640]{1,0:T(8,128)(2,1)S(1)}, bf16[256,640]{1,0:T(8,128)(2,1)S(1)}, u32[]{:S(2)}, u32[]{:S(2)}) collective-permute-start(bf16[256,640]{1,0:T(8,128)(2,1)S(1)} %get-tuple-element.42), channel_id=1, source_target_pairs={{2,0},{3,1},{4,2},{5,3},{6,4},{7,5},{0,6},{1,7},{10,8},{11,9},{12,... | collective-permute-start | bytes 983048 | tf_op jit(solution)/shard_map/ppermute | solution.py:52
  155.5 30.5 %collective-permute-start.24 = (bf16[4,128,640]{2,1,0:T(8,128)(2,1)S(1)}, bf16[4,128,640]{2,1,0:T(8,128)(2,1)S(1)}, u32[]{:S(2)}, u32[]{:S(2)}) collective-permute-start(bf16[4,128,640]{2,1,0:T(8,128)(2,1)S(1)} %shard_map.97), channel_id=1, source_target_pairs={{0,1},{1,0},{2,3},{3,2},{4,5},{5,4},{6,7},{7,6},{8,9},{9,8},{10,11... | collective-permute-start | bytes 1966088 | tf_op jit(solution)/shard_map/ppermute | solution.py:52
  158.1 13.0 %collective-permute-start.15 = (bf16[128,640]{1,0:T(8,128)(2,1)S(1)}, bf16[128,640]{1,0:T(8,128)(2,1)S(1)}, u32[]{:S(2)}, u32[]{:S(2)}) collective-permute-start(bf16[128,640]{1,0:T(8,128)(2,1)S(1)} %get-tuple-element.37), channel_id=1, source_target_pairs={{0,0},{1,1},{2,2},{3,3},{4,4},{5,5},{6,6},{7,7},{8,8},{9,9},{10,10... | collective-permute-start | bytes 491528 | tf_op jit(solution)/shard_map/ppermute | solution.py:52
  160.0 11.1 %collective-permute-start.16 = (bf16[128,640]{1,0:T(8,128)(2,1)S(1)}, bf16[128,640]{1,0:T(8,128)(2,1)S(1)}, u32[]{:S(2)}, u32[]{:S(2)}) collective-permute-start(bf16[128,640]{1,0:T(8,128)(2,1)S(1)} %get-tuple-element.38), channel_id=1, source_target_pairs={{2,0},{3,1},{4,2},{5,3},{6,4},{7,5},{0,6},{1,7},{10,8},{11,9},{12,... | collective-permute-start | bytes 491528 | tf_op jit(solution)/shard_map/ppermute | solution.py:52
  162.0 11.5 %collective-permute-start.17 = (bf16[128,640]{1,0:T(8,128)(2,1)S(1)}, bf16[128,640]{1,0:T(8,128)(2,1)S(1)}, u32[]{:S(2)}, u32[]{:S(2)}) collective-permute-start(bf16[128,640]{1,0:T(8,128)(2,1)S(1)} %get-tuple-element.39), channel_id=1, source_target_pairs={{4,0},{5,1},{6,2},{7,3},{0,4},{1,5},{2,6},{3,7},{12,8},{13,9},{14,... | collective-permute-start | bytes 491528 | tf_op jit(solution)/shard_map/ppermute | solution.py:52
  166.9 16.7 %collective-permute-start.18 = (bf16[128,640]{1,0:T(8,128)(2,1)S(1)}, bf16[128,640]{1,0:T(8,128)(2,1)S(1)}, u32[]{:S(2)}, u32[]{:S(2)}) collective-permute-start(bf16[128,640]{1,0:T(8,128)(2,1)S(1)} %get-tuple-element.40), channel_id=1, source_target_pairs={{6,0},{7,1},{0,2},{1,3},{2,4},{3,5},{4,6},{5,7},{14,8},{15,9},{8,1... | collective-permute-start | bytes 491528 | tf_op jit(solution)/shard_map/ppermute | solution.py:52
  183.6 4.1 %collective-permute-start.19 = (bf16[4,64,640]{2,1,0:T(8,128)(2,1)S(1)}, bf16[4,64,640]{2,1,0:T(8,128)(2,1)S(1)}, u32[]{:S(2)}, u32[]{:S(2)}) collective-permute-start(bf16[4,64,640]{2,1,0:T(8,128)(2,1)S(1)} %shard_map.95), channel_id=1, source_target_pairs={{0,1},{1,0},{2,3},{3,2},{4,5},{5,4},{6,7},{7,6},{8,9},{9,8},{10,11... | collective-permute-start | bytes 983048 | tf_op jit(solution)/shard_map/ppermute | solution.py:52

commit v2 on v1

v2 whole, which is shorter than its diff:
```python
import functools

import jax
import jax.numpy as jnp
from jax import lax
from jax.experimental import pallas as pl
from jax.experimental.pallas import tpu as pltpu
from jax.sharding import PartitionSpec as P

F32 = jnp.float32
LOW = jnp.bfloat16
AXES = ("blk", "uly")
CHIPS = 4
RING = 8
PAD = 16


def shift(b, core):
    return (b // RING % 2) * core


def gather_pairs(blocks, d):
    return [(b * 8 + u, b * 8 + (u + 2 * d) % 8) for b in range(blocks) for u in range(8)]


def next_pairs(blocks):
    pairs = []
    for b in range(blocks):
        after = (b + 1) % blocks
        for u in range(8):
            chip, core = u // 2, u % 2
            chip = (chip + shift(b, core) - shift(after, core)) % CHIPS
            pairs.append((b * 8 + u, after * 8 + 2 * chip + core))
    return pairs


def hop_pairs(blocks):
    pairs = []
    for s, t in next_pairs(blocks):
        b = s // 8
        pairs.append((s, (b ^ RING) * 8 + t % 8 if b % RING == RING - 1 else s))
    return pairs


def after_hop_pairs(blocks):
    onward = dict(next_pairs(blocks))
    return [(t, onward[s]) for s, t in hop_pairs(blocks)]


def back(pairs):
    return [(t, s) for s, t in pairs]


def core_pairs(blocks):
    return [(i, i ^ 1) for i in range(blocks * 8)]


def moved(value, pairs):
    if all(s == t for s, t in pairs):
        return value
    return lax.ppermute(value, AXES, pairs)


def whole(n):
    return [pl.BlockSpec(memory_space=pltpu.VMEM)] * n


def columns(group, width):
    return pl.ds(pl.multiple_of(group * width, 128), width)


def call(kernel, out_shape, place, *arrays, after=()):
    moved_bytes = sum(a.size * a.dtype.itemsize for a in arrays)
    outs = out_shape if isinstance(out_shape, (list, tuple)) else [out_shape]
    moved_bytes += sum(o.size * o.dtype.itemsize for o in outs)
    waits = len(after)

    def body(place_ref, *refs):
        kernel(place_ref, *refs[waits:])

    return pl.pallas_call(
        body,
        out_shape=out_shape,
        in_specs=[pl.BlockSpec(memory_space=pltpu.SMEM)]
        + [pl.BlockSpec(memory_space=pl.ANY)] * waits
        + whole(len(arrays)),
        out_specs=jax.tree.map(lambda _: pl.BlockSpec(memory_space=pltpu.VMEM), out_shape),
        compiler_params=pltpu.CompilerParams(vmem_limit_bytes=32 << 20),
        cost_estimate=pl.CostEstimate(flops=0, bytes_accessed=moved_bytes, transcendentals=0),
    )(place, *after, *arrays)


def joined(parts, place, after=()):
    length, width = parts[0].shape

    def kernel(place_ref, *refs):
        for i in range(len(parts)):
            refs[-1][i * length : (i + 1) * length] = refs[i][...]

    return call(kernel, jax.ShapeDtypeStruct((len(parts) * length, width), LOW), place, *parts, after=after)


def other_core_parts(first, second, stats, place):
    rows, width = first.shape[0], first.shape[1] // 8
    extra = PAD if stats is not None else 0

    def kernel(place_ref, a_ref, b_ref, *refs):
        out_ref = refs[-1]
        for d in range(CHIPS):
            group = 2 * lax.rem(place_ref[1] + d, CHIPS) + 1 - place_ref[2]
            out_ref[d, :rows] = a_ref[:, columns(group, width)]
            out_ref[d, rows : 2 * rows] = b_ref[:, columns(group, width)]
            if extra:
                out_ref[d, 2 * rows :] = refs[0][group]

    arrays = (first, second) + ((stats,) if extra else ())
    shape = jax.ShapeDtypeStruct((CHIPS, 2 * rows + extra, width), LOW)
    return call(kernel, shape, place, *arrays)


def messages(first, second, stats, other, place, which, after=()):
    rows, width = first.shape[0], first.shape[1] // 8
    extra = PAD if stats is not None else 0

    def kernel(place_ref, a_ref, b_ref, *refs):
        other_ref, outs = refs[-len(which) - 1], refs[-len(which) :]
        for d, out_ref in zip(which, outs):
            group = 2 * lax.rem(place_ref[0] + d, CHIPS) + place_ref[2]
            out_ref[:rows] = a_ref[:, columns(group, width)]
            out_ref[rows : 2 * rows] = b_ref[:, columns(group, width)]
            out_ref[2 * rows : 4 * rows] = other_ref[d, : 2 * rows]
            if extra:
                out_ref[4 * rows :] = jnp.concatenate(
                    [refs[0][group, : PAD // 2], other_ref[d, 2 * rows : 2 * rows + PAD // 2]], axis=0
                )

    arrays = (first, second) + ((stats,) if extra else ()) + (other,)
    shape = [jax.ShapeDtypeStruct((4 * rows + extra, width), LOW)] * len(which)
    return call(kernel, shape, place, *arrays, after=after)


def nt(a, b):
    return lax.dot_general(a, b, (((1,), (1,)), ((), ())), preferred_element_type=F32)


def nn(a, b):
    return lax.dot_general(a, b, (((1,), (0,)), ((), ())), preferred_element_type=F32)


def tn(a, b):
    return lax.dot_general(a, b, (((0,), (0,)), ((), ())), preferred_element_type=F32)


def grads(queries, keys, work, sums_in, outputs, rows, heads, scale):
    width = keys[0].shape[1]
    head = width // heads
    size = 4 * rows + PAD
    ins, outs = list(sums_in), list(outputs)

    def kernel(*refs):
        query_refs = refs[: len(queries)]
        key_refs = refs[len(queries) : len(queries) + len(keys)]
        in_refs = dict(zip(ins, refs[len(queries) + len(keys) :]))
        out_refs = dict(zip(outs, refs[len(queries) + len(keys) + len(ins) :]))
        def part(ref, top, which):
            starts = [top + (2 * e + which) * rows for e in range(2)]
            return [ref[t : t + rows] for t in starts]

        total = {}
        for (kind, i), ref in in_refs.items():
            if kind == "q":
                total[kind, i] = ref[...]
            else:
                total["k", i] = jnp.concatenate(part(ref, 0, 0), axis=0)
                total["v", i] = jnp.concatenate(part(ref, 0, 1), axis=0)

        def add(kind, i, value):
            total[kind, i] = total[kind, i] + value if (kind, i) in total else value

        def rows_of(refs, tops, which):
            return jnp.concatenate([x for r in refs for t in tops for x in part(r, t, which)], axis=0)

        for queries_here, keys_here in work:
            sources = [query_refs[i] for i in queries_here]
            q = rows_of(sources, (0, size), 0)
            g = rows_of(sources, (0, size), 1)
            stats = []
            for ref in sources:
                for top in (0, size):
                    pad = ref[top + 4 * rows : top + size].astype(F32)
                    stats += [pad[:1], pad[PAD // 2 : PAD // 2 + 1]]
            sums = jnp.concatenate([s[:, :rows] for s in stats], axis=1)
            deltas = jnp.concatenate([s[:, rows:] for s in stats], axis=1)
            k = rows_of([key_refs[d] for d in keys_here], (0,), 0)
            v = rows_of([key_refs[d] for d in keys_here], (0,), 1)
            prob = jnp.exp(nt(k, q) * scale - sums)
            score_grad = (prob * (nt(v, g) - deltas)).astype(LOW)
            gv = nn(prob.astype(LOW), g)
            gk = nn(score_grad, q)
            gq = tn(score_grad, k)
            for n, d in enumerate(keys_here):
                at = slice(2 * n * rows, 2 * (n + 1) * rows)
                add("k", d, gk[at])
                add("v", d, gv[at])
            for n, i in enumerate(queries_here):
                add("q", i, gq[4 * n * rows : 4 * (n + 1) * rows])
        for (kind, i), ref in out_refs.items():
            by = scale if ref.dtype == LOW else 1.0
            if kind == "q":
                ref[...] = (total[kind, i] * by).astype(ref.dtype)
                continue
            for e in range(2):
                at = slice(e * rows, (e + 1) * rows)
                ref[2 * e * rows : (2 * e + 1) * rows] = (total["k", i][at] * by).astype(ref.dtype)
                ref[(2 * e + 1) * rows : (2 * e + 2) * rows] = total["v", i][at].astype(ref.dtype)

    def block(length):
        return pl.BlockSpec((length, head), lambda h: (0, h))

    shapes = [jax.ShapeDtypeStruct((4 * rows, width), outputs[name]) for name in outs]
    pairs = heads * 8 * rows * rows * sum(len(a) * len(b) for a, b in work)
    results = pl.pallas_call(
        kernel,
        grid=(heads,),
        in_specs=[block(2 * size)] * len(queries) + [block(4 * rows)] * (len(keys) + len(ins)),
        out_specs=[block(4 * rows)] * len(outs),
        out_shape=shapes,
        compiler_params=pltpu.CompilerParams(
            dimension_semantics=("arbitrary",), vmem_limit_bytes=40 << 20
        ),
        cost_estimate=pl.CostEstimate(
            flops=10 * pairs * head, bytes_accessed=8 << 20, transcendentals=pairs
        ),
    )(*queries, *keys, *sums_in.values())
    return dict(zip(outs, results))


def query_sums(own, returned, rows, scale, place):
    def kernel(place_ref, own_ref, back_ref, *outs):
        for i in range(2):
            at = slice(2 * i * rows, (2 * i + 2) * rows)
            outs[i][...] = (own_ref[at, :] * scale + back_ref[at, :].astype(F32)).astype(LOW)

    shape = [jax.ShapeDtypeStruct((2 * rows, own.shape[1]), LOW)] * 2
    return call(kernel, shape, place, own, returned)


def cross_parts(parts, place, after=()):
    shape = jax.ShapeDtypeStruct((CHIPS, parts[0].shape[0] // 2, parts[0].shape[1]), LOW)

    def kernel(place_ref, *refs):
        half = shape.shape[1]
        for d in range(CHIPS):
            refs[-1][d] = refs[d][half:]

    return call(kernel, shape, place, *parts, after=after)


def spread(parts, other, place, rows, count):
    width = parts[0].shape[1]

    def kernel(place_ref, *refs):
        other_ref, outs = refs[CHIPS], refs[CHIPS + 1 :]
        for d in range(CHIPS):
            mine = 2 * lax.rem(place_ref[0] + d, CHIPS) + place_ref[2]
            others = 2 * lax.rem(place_ref[1] + d, CHIPS) + 1 - place_ref[2]
            for i in range(count):
                at = slice(i * rows, (i + 1) * rows)
                outs[i][:, columns(mine, width)] = refs[d][at]
                outs[i][:, columns(others, width)] = other_ref[d, at]

    shape = [jax.ShapeDtypeStruct((rows, 8 * width), LOW)] * count
    return call(kernel, shape, place, *parts, other)


def per_device(blocks, query_rows, key_rows, value_rows, out_grad, log_sums, deltas):
    rows, heads_total = log_sums.shape
    heads = heads_total // 8
    width = query_rows.shape[1] // 8
    scale = (width // heads) ** (-0.5)
    chip, core = lax.axis_index("uly") // 2, lax.axis_index("uly") % 2
    block = lax.axis_index("blk")
    place = jnp.stack([chip + shift(block, core), chip + shift(block, 1 - core), core]).astype(jnp.int32)
    stats = jnp.concatenate([log_sums.T, deltas.T], axis=1).reshape(8, 1, width)
    stats = jnp.pad(stats, ((0, 0), (0, PAD - 1), (0, 0)))

    cores = core_pairs(blocks)
    there = [gather_pairs(blocks, d) for d in range(CHIPS)]
    home = [back(pairs) for pairs in there]
    onward = next_pairs(blocks)
    hop, after_hop = hop_pairs(blocks), after_hop_pairs(blocks)

    other = moved(other_core_parts(query_rows, out_grad, stats, place), cores)
    other_keys = moved(other_core_parts(key_rows, value_rows, None, place), cores)
    sent = messages(query_rows, out_grad, stats, other, place, range(CHIPS))
    own = [moved(m, there[d]) for d, m in enumerate(sent)]
    queries = [joined((own[0], own[1]), place)]
    before = [moved(queries[0], onward)]

    near = messages(key_rows, value_rows, None, other_keys, place, (1, 3), ())
    near_keys = [moved(m, there[d]) for d, m in zip((1, 3), near)]
    queries.append(joined((own[3], own[2]), place, tuple(near_keys)))
    before.append(moved(queries[1], onward))
    rest = messages(key_rows, value_rows, None, other_keys, place, (0, 2), (own[1],))
    keys = [rest[0], near_keys[0], moved(rest[1], there[2]), near_keys[1]]

    early = (0, 1, 3)
    mine = [("q", 0), ("q", 1), ("q", 2)]
    so_far = grads(
        [*queries, before[0]], [keys[d] for d in early], [((i,), (0, 1, 2)) for i in range(3)],
        {}, {name: F32 for name in mine + [("kv", 0), ("kv", 1), ("kv", 2)]}, rows, heads, scale,
    )
    more = grads(
        [before[1]], [keys[d] for d in early], [((0,), (0, 1, 2))],
        {("kv", n): so_far["kv", n] for n in range(3)},
        {("q", 0): F32, ("kv", 0): LOW, ("kv", 1): LOW, ("kv", 2): LOW}, rows, heads, scale,
    )
    last = grads(
        [*queries, *before], [keys[2]], [((0, 1), (0,)), ((2, 3), (0,))],
        {**{name: so_far[name] for name in mine}, ("q", 3): more["q", 0]},
        {("q", 0): F32, ("q", 1): F32, ("q", 2): LOW, ("q", 3): LOW, ("kv", 0): LOW}, rows, heads, scale,
    )
    key_grads = [more["kv", 0], more["kv", 1], last["kv", 0], more["kv", 2]]
    done = last
    returned = [
        moved(done["q", 2], back(onward)),
        moved(done["q", 3], back(onward)),
    ]
    key_home = [moved(m, home[d]) for d, m in enumerate(key_grads)]
    grad_0, grad_1 = query_sums(done["q", 0], returned[0], rows, scale, place)
    grad_3, grad_2 = query_sums(done["q", 1], returned[1], rows, scale, place)
    query_home = [moved(m, home[d]) for d, m in enumerate((grad_0, grad_1, grad_2, grad_3))]

    other = moved(cross_parts(key_home, place, tuple(query_home[1:])), cores)
    out_k, out_v = spread(key_home, other, place, rows, 2)
    other = moved(cross_parts(query_home, place), cores)
    (out_q,) = spread(query_home, other, place, rows, 1)
    return out_q, out_k, out_v


def solution(mesh):
    rows = P(AXES, None)
    return jax.shard_map(
        functools.partial(per_device, mesh.shape["blk"]),
        mesh=mesh,
        in_specs=(rows,) * 6,
        out_specs=(rows,) * 3,
        check_vma=False,
    )
```

time: 190 us -> 178 us (0.937)
  the two profiles are of different devices: /device:TPU:57 before, /device:TPU:6 now
where the time goes in v2:
time: 178 us; the launch traced here: 175 us
  starting transfers between devices  74 us (42%)
  waiting for transfers between devices  71.6 us (40%)
  Pallas kernels  24.9 us (14%)
  local copies, waits for them, and re-layouts  2.91 us (2%)
    ppermute x20, starting transfers between devices, moved(): return lax.ppermute(value, AXES, pairs)  74 us
    ppermute x20, waiting for transfers between devices, moved(): return lax.ppermute(value, AXES, pairs)  71.6 us
    pallas_call x3, Pallas kernels, grads(): pl.pallas_call(kernel, grid=(heads,), in_specs=[block(2 * size)] * len(qu...  15 us
    pallas_call x13, Pallas kernels, call(): pl.pallas_call(body, out_shape=out_shape, in_specs=[pl.BlockSpec(memory_s...  9.81 us
  transfers between devices with their start and end apart: 20, of which 6 were waited for; matrix products, arithmetic and copies ran while one was open for 0% of the time, Pallas kernels for 10%

profile of v2, /device:TPU:6, one launch (start us, length us, event | category | flops | bytes accessed | tf_op | source)
XLA Modules:
  0.0 174.5 jit_solution(6743587297382688443)
XLA Ops:
  0.7 0.0 copy-start.5
  0.7 0.0 copy-start.4
  0.7 0.7 copy-done.5
  1.4 0.0 copy-done.4
  1.4 0.1 pad_maximum_fusion
  1.5 0.1 pad_add_fusion.place_ref
  1.6 1.1 copy-done.2
  2.7 1.1 copy-done.3
  3.8 0.6 shard_map.85
  4.4 1.9 %collective-permute-start = (bf16[4,144,640]{2,1,0:T(8,128)(2,1)S(1)}, bf16[4,144,640]{2,1,0:T(8,128)(2,1)S(1)}, u32[]{:S(2)}, u32[]{:S(2)}) collective-permute-start(bf16[4,144,640]{2,1,0:T(8,128)(2,1)S(1)} %shard_map.85), channel_id=1, source_target_pairs={{0,1},{1,0},{2,3},{3,2},{4,5},{5,4},{6,7},{7,6},{8,9},{9,8},{10,11... | collective-permute-start | bytes 2211848 | tf_op jit(solution)/shard_map/ppermute | solution.py:61
  6.3 0.6 shard_map.88
  6.9 2.4 %collective-permute-start.2 = (bf16[4,128,640]{2,1,0:T(8,128)(2,1)S(1)}, bf16[4,128,640]{2,1,0:T(8,128)(2,1)S(1)}, u32[]{:S(2)}, u32[]{:S(2)}) collective-permute-start(bf16[4,128,640]{2,1,0:T(8,128)(2,1)S(1)} %shard_map.88), channel_id=1, source_target_pairs={{0,1},{1,0},{2,3},{3,2},{4,5},{5,4},{6,7},{7,6},{8,9},{9,8},{10,11... | collective-permute-start | bytes 1966088 | tf_op jit(solution)/shard_map/ppermute | solution.py:61
  9.4 0.0 collective-permute-done.refs_3_
  9.4 0.7 shard_map.86
  10.0 6.1 %collective-permute-start.1 = (bf16[272,640]{1,0:T(8,128)(2,1)S(1)}, bf16[272,640]{1,0:T(8,128)(2,1)S(1)}, u32[]{:S(2)}, u32[]{:S(2)}) collective-permute-start(bf16[272,640]{1,0:T(8,128)(2,1)S(1)} %get-tuple-element.33), channel_id=1, source_target_pairs={{0,2},{1,3},{2,4},{3,5},{4,6},{5,7},{6,0},{7,1},{8,10},{9,11},{10,... | collective-permute-start | bytes 1044488 | tf_op jit(solution)/shard_map/ppermute | solution.py:61
  16.1 6.8 %collective-permute-start.5 = (bf16[272,640]{1,0:T(8,128)(2,1)S(1)}, bf16[272,640]{1,0:T(8,128)(2,1)S(1)}, u32[]{:S(2)}, u32[]{:S(2)}) collective-permute-start(bf16[272,640]{1,0:T(8,128)(2,1)S(1)} %get-tuple-element.36), channel_id=1, source_target_pairs={{0,6},{1,7},{2,0},{3,1},{4,2},{5,3},{6,4},{7,5},{8,14},{9,15},{10,... | collective-permute-start | bytes 1044488 | tf_op jit(solution)/shard_map/ppermute | solution.py:61
  22.9 6.0 %collective-permute-start.6 = (bf16[272,640]{1,0:T(8,128)(2,1)S(1)}, bf16[272,640]{1,0:T(8,128)(2,1)S(1)}, u32[]{:S(2)}, u32[]{:S(2)}) collective-permute-start(bf16[272,640]{1,0:T(8,128)(2,1)S(1)} %get-tuple-element.37), channel_id=1, source_target_pairs={{0,4},{1,5},{2,6},{3,7},{4,0},{5,1},{6,2},{7,3},{8,12},{9,13},{10,... | collective-permute-start | bytes 1044488 | tf_op jit(solution)/shard_map/ppermute | solution.py:61
  28.9 0.0 collective-permute-done.2.refs_2_.refs_3_
  28.9 0.6 shard_map.89
  29.5 3.1 %collective-permute-start.3 = (bf16[256,640]{1,0:T(8,128)(2,1)S(1)}, bf16[256,640]{1,0:T(8,128)(2,1)S(1)}, u32[]{:S(2)}, u32[]{:S(2)}) collective-permute-start(bf16[256,640]{1,0:T(8,128)(2,1)S(1)} %get-tuple-element.34), channel_id=1, source_target_pairs={{0,2},{1,3},{2,4},{3,5},{4,6},{5,7},{6,0},{7,1},{8,10},{9,11},{10,... | collective-permute-start | bytes 983048 | tf_op jit(solution)/shard_map/ppermute | solution.py:61
  32.6 4.9 %collective-permute-start.4 = (bf16[256,640]{1,0:T(8,128)(2,1)S(1)}, bf16[256,640]{1,0:T(8,128)(2,1)S(1)}, u32[]{:S(2)}, u32[]{:S(2)}) collective-permute-start(bf16[256,640]{1,0:T(8,128)(2,1)S(1)} %get-tuple-element.35), channel_id=1, source_target_pairs={{0,6},{1,7},{2,0},{3,1},{4,2},{5,3},{6,4},{7,5},{8,14},{9,15},{10,... | collective-permute-start | bytes 983048 | tf_op jit(solution)/shard_map/ppermute | solution.py:61
  37.5 0.0 collective-permute-done.1.refs_1_.refs_0_
  37.5 0.6 shard_map.87.refs_0_
  38.1 3.5 %collective-permute-start.7 = (bf16[544,640]{1,0:T(8,128)(2,1)S(1)}, bf16[544,640]{1,0:T(8,128)(2,1)S(1)}, u32[]{:S(2)}, u32[]{:S(2)}) collective-permute-start(bf16[544,640]{1,0:T(8,128)(2,1)S(1)} %shard_map.87.refs_0_), channel_id=1, source_target_pairs={{0,8},{1,9},{2,10},{3,11},{4,12},{5,13},{6,14},{7,15},{8,16},{9,17... | collective-permute-start | bytes 2088968 | tf_op jit(solution)/shard_map/ppermute | solution.py:61
  41.6 36.2 %collective-permute-done.3.refs_0_.refs_4_.refs_2_ = bf16[256,640]{1,0:T(8,128)(2,1)S(1)} collective-permute-done((bf16[256,640]{1,0:T(8,128)(2,1)S(1)}, bf16[256,640]{1,0:T(8,128)(2,1)S(1)}, u32[]{:S(2)}, u32[]{:S(2)}) %collective-permute-start.3) | collective-permute-done | bytes 327712 | tf_op jit(solution)/shard_map/ppermute | solution.py:61
  77.8 0.0 collective-permute-done.4.refs_1_.refs_5_.refs_3_
  77.8 0.0 collective-permute-done.5.refs_2_
  77.8 0.0 collective-permute-done.6.refs_3_
  77.8 0.6 shard_map.90.refs_1_
  78.4 1.9 %collective-permute-start.8 = (bf16[544,640]{1,0:T(8,128)(2,1)S(1)}, bf16[544,640]{1,0:T(8,128)(2,1)S(1)}, u32[]{:S(2)}, u32[]{:S(2)}) collective-permute-start(bf16[544,640]{1,0:T(8,128)(2,1)S(1)} %shard_map.90.refs_1_), channel_id=1, source_target_pairs={{0,8},{1,9},{2,10},{3,11},{4,12},{5,13},{6,14},{7,15},{8,16},{9,17... | collective-permute-start | bytes 2088968 | tf_op jit(solution)/shard_map/ppermute | solution.py:61
  80.4 0.6 shard_map.91
  81.0 5.0 %collective-permute-start.9 = (bf16[256,640]{1,0:T(8,128)(2,1)S(1)}, bf16[256,640]{1,0:T(8,128)(2,1)S(1)}, u32[]{:S(2)}, u32[]{:S(2)}) collective-permute-start(bf16[256,640]{1,0:T(8,128)(2,1)S(1)} %get-tuple-element.38), channel_id=1, source_target_pairs={{0,4},{1,5},{2,6},{3,7},{4,0},{5,1},{6,2},{7,3},{8,12},{9,13},{10,... | collective-permute-start | bytes 983048 | tf_op jit(solution)/shard_map/ppermute | solution.py:61
  86.0 0.0 collective-permute-done.7.refs_2_
  86.0 6.8 %shard_map.92 = (f32[256,640]{1,0:T(8,128)S(1)}, f32[256,640]{1,0:T(8,128)S(1)}, f32[256,640]{1,0:T(8,128)S(1)}, f32[256,640]{1,0:T(8,128)S(1)}, f32[256,640]{1,0:T(8,128)S(1)}, /*index=5*/f32[256,640]{1,0:T(8,128)S(1)}) custom-call(bf16[544,640]{1,0:T(8,128)(2,1)S(1)} %shard_map.87.refs_0_, bf16[544,640]{1,0:T(8,128)(2,1)S(1)} %shard_map.90.refs_1_, ...), custom_call_target="tpu_custom_call" | custom-call | flops 1887436800 | bytes 8388608 | tf_op jit(solution)/shard_map/pallas_call | solution.py:222
  92.8 8.7 %collective-permute-done.8.refs_0_.refs_3_ = bf16[544,640]{1,0:T(8,128)(2,1)S(1)} collective-permute-done((bf16[544,640]{1,0:T(8,128)(2,1)S(1)}, bf16[544,640]{1,0:T(8,128)(2,1)S(1)}, u32[]{:S(2)}, u32[]{:S(2)}) %collective-permute-start.8) | collective-permute-done | bytes 696352 | tf_op jit(solution)/shard_map/ppermute | solution.py:61
  101.4 3.4 %shard_map.93 = (f32[256,640]{1,0:T(8,128)S(1)}, bf16[256,640]{1,0:T(8,128)(2,1)S(1)}, bf16[256,640]{1,0:T(8,128)(2,1)S(1)}, bf16[256,640]{1,0:T(8,128)(2,1)S(1)}) custom-call(bf16[544,640]{1,0:T(8,128)(2,1)S(1)} %collective-permute-done.8.refs_0_.refs_3_, bf16[256,640]{1,0:T(8,128)(2,1)S(1)} %get-tuple-element.39.refs_3_.refs_1_, ...), custom_call_target="tpu_custom_call" | custom-call | flops 629145600 | bytes 8388608 | tf_op jit(solution)/shard_map/pallas_call | solution.py:222
  104.8 4.1 %collective-permute-done.9.refs_4_ = bf16[256,640]{1,0:T(8,128)(2,1)S(1)} collective-permute-done((bf16[256,640]{1,0:T(8,128)(2,1)S(1)}, bf16[256,640]{1,0:T(8,128)(2,1)S(1)}, u32[]{:S(2)}, u32[]{:S(2)}) %collective-permute-start.9) | collective-permute-done | bytes 327712 | tf_op jit(solution)/shard_map/ppermute | solution.py:61
  108.9 4.9 %shard_map.94 = (f32[256,640]{1,0:T(8,128)S(1)}, f32[256,640]{1,0:T(8,128)S(1)}, bf16[256,640]{1,0:T(8,128)(2,1)S(1)}, bf16[256,640]{1,0:T(8,128)(2,1)S(1)}, bf16[256,640]{1,0:T(8,128)(2,1)S(1)}) custom-call(bf16[544,640]{1,0:T(8,128)(2,1)S(1)} %shard_map.87.refs_0_, bf16[544,640]{1,0:T(8,128)(2,1)S(1)} %shard_map.90.refs_1_, ...), custom_call_target="tpu_custom_call" | custom-call | flops 838860800 | bytes 8388608 | tf_op jit(solution)/shard_map/pallas_call | solution.py:222
  113.8 1.9 %collective-permute-start.10 = (bf16[256,640]{1,0:T(8,128)(2,1)S(1)}, bf16[256,640]{1,0:T(8,128)(2,1)S(1)}, u32[]{:S(2)}, u32[]{:S(2)}) collective-permute-start(bf16[256,640]{1,0:T(8,128)(2,1)S(1)} %get-tuple-element.48), channel_id=1, source_target_pairs={{8,0},{9,1},{10,2},{11,3},{12,4},{13,5},{14,6},{15,7},{16,8},{17,9... | collective-permute-start | bytes 983048 | tf_op jit(solution)/shard_map/ppermute | solution.py:61
  115.7 1.9 %collective-permute-start.12 = (bf16[256,640]{1,0:T(8,128)(2,1)S(1)}, bf16[256,640]{1,0:T(8,128)(2,1)S(1)}, u32[]{:S(2)}, u32[]{:S(2)}) collective-permute-start(bf16[256,640]{1,0:T(8,128)(2,1)S(1)} %get-tuple-element.52), channel_id=1, source_target_pairs={{8,0},{9,1},{10,2},{11,3},{12,4},{13,5},{14,6},{15,7},{16,8},{17,9... | collective-permute-start | bytes 983048 | tf_op jit(solution)/shard_map/ppermute | solution.py:61
  117.6 4.0 %collective-permute-start.17 = (bf16[256,640]{1,0:T(8,128)(2,1)S(1)}, bf16[256,640]{1,0:T(8,128)(2,1)S(1)}, u32[]{:S(2)}, u32[]{:S(2)}) collective-permute-start(bf16[256,640]{1,0:T(8,128)(2,1)S(1)} %get-tuple-element.57), channel_id=1, source_target_pairs={{4,0},{5,1},{6,2},{7,3},{0,4},{1,5},{2,6},{3,7},{12,8},{13,9},{14,... | collective-permute-start | bytes 983048 | tf_op jit(solution)/shard_map/ppermute | solution.py:61
  121.6 3.5 %collective-permute-start.16 = (bf16[256,640]{1,0:T(8,128)(2,1)S(1)}, bf16[256,640]{1,0:T(8,128)(2,1)S(1)}, u32[]{:S(2)}, u32[]{:S(2)}) collective-permute-start(bf16[256,640]{1,0:T(8,128)(2,1)S(1)} %get-tuple-element.56), channel_id=1, source_target_pairs={{2,0},{3,1},{4,2},{5,3},{6,4},{7,5},{0,6},{1,7},{10,8},{11,9},{12,... | collective-permute-start | bytes 983048 | tf_op jit(solution)/shard_map/ppermute | solution.py:61
  125.1 3.4 %collective-permute-start.18 = (bf16[256,640]{1,0:T(8,128)(2,1)S(1)}, bf16[256,640]{1,0:T(8,128)(2,1)S(1)}, u32[]{:S(2)}, u32[]{:S(2)}) collective-permute-start(bf16[256,640]{1,0:T(8,128)(2,1)S(1)} %get-tuple-element.58), channel_id=1, source_target_pairs={{6,0},{7,1},{0,2},{1,3},{2,4},{3,5},{4,6},{5,7},{14,8},{15,9},{8,1... | collective-permute-start | bytes 983048 | tf_op jit(solution)/shard_map/ppermute | solution.py:61
  128.5 0.0 collective-permute-done.10.refs_1_
  128.5 0.6 shard_map.95
  129.1 4.6 %collective-permute-start.11 = (bf16[128,640]{1,0:T(8,128)(2,1)S(1)}, bf16[128,640]{1,0:T(8,128)(2,1)S(1)}, u32[]{:S(2)}, u32[]{:S(2)}) collective-permute-start(bf16[128,640]{1,0:T(8,128)(2,1)S(1)} %get-tuple-element.50), channel_id=1, source_target_pairs={{2,0},{3,1},{4,2},{5,3},{6,4},{7,5},{0,6},{1,7},{10,8},{11,9},{12,... | collective-permute-start | bytes 491528 | tf_op jit(solution)/shard_map/ppermute | solution.py:61
  133.7 0.0 collective-permute-done.12.refs_1_
  133.8 0.6 shard_map.96
  134.4 6.9 %collective-permute-start.13 = (bf16[128,640]{1,0:T(8,128)(2,1)S(1)}, bf16[128,640]{1,0:T(8,128)(2,1)S(1)}, u32[]{:S(2)}, u32[]{:S(2)}) collective-permute-start(bf16[128,640]{1,0:T(8,128)(2,1)S(1)} %get-tuple-element.53), channel_id=1, source_target_pairs={{4,0},{5,1},{6,2},{7,3},{0,4},{1,5},{2,6},{3,7},{12,8},{13,9},{14,... | collective-permute-start | bytes 491528 | tf_op jit(solution)/shard_map/ppermute | solution.py:61
  141.3 0.0 collective-permute-done.17.refs_5_.refs_2_
  141.3 1.9 %collective-permute-start.14 = (bf16[128,640]{1,0:T(8,128)(2,1)S(1)}, bf16[128,640]{1,0:T(8,128)(2,1)S(1)}, u32[]{:S(2)}, u32[]{:S(2)}) collective-permute-start(bf16[128,640]{1,0:T(8,128)(2,1)S(1)} %get-tuple-element.54), channel_id=1, source_target_pairs={{6,0},{7,1},{0,2},{1,3},{2,4},{3,5},{4,6},{5,7},{14,8},{15,9},{8,1... | collective-permute-start | bytes 491528 | tf_op jit(solution)/shard_map/ppermute | solution.py:61
  143.3 17.9 %collective-permute-done.16.refs_4_.refs_1_ = bf16[256,640]{1,0:T(8,128)(2,1)S(1)} collective-permute-done((bf16[256,640]{1,0:T(8,128)(2,1)S(1)}, bf16[256,640]{1,0:T(8,128)(2,1)S(1)}, u32[]{:S(2)}, u32[]{:S(2)}) %collective-permute-start.16) | collective-permute-done | bytes 327712 | tf_op jit(solution)/shard_map/ppermute | solution.py:61
  161.2 0.0 collective-permute-done.18.refs_6_.refs_3_
  161.2 3.4 %collective-permute-done.11.refs_1_.refs_0_ = bf16[128,640]{1,0:T(8,128)(2,1)S(1)} collective-permute-done((bf16[128,640]{1,0:T(8,128)(2,1)S(1)}, bf16[128,640]{1,0:T(8,128)(2,1)S(1)}, u32[]{:S(2)}, u32[]{:S(2)}) %collective-permute-start.11) | collective-permute-done | bytes 163872 | tf_op jit(solution)/shard_map/ppermute | solution.py:61
  164.6 0.0 collective-permute-done.13.refs_2_.refs_1_
  164.6 0.0 collective-permute-done.14.refs_3_.refs_2_
  164.6 0.6 shard_map.99
  165.2 1.9 %collective-permute-start.19 = (bf16[4,128,640]{2,1,0:T(8,128)(2,1)S(1)}, bf16[4,128,640]{2,1,0:T(8,128)(2,1)S(1)}, u32[]{:S(2)}, u32[]{:S(2)}) collective-permute-start(bf16[4,128,640]{2,1,0:T(8,128)(2,1)S(1)} %shard_map.99), channel_id=1, source_target_pairs={{0,1},{1,0},{2,3},{3,2},{4,5},{5,4},{6,7},{7,6},{8,9},{9,8},{10,11... | collective-permute-start | bytes 1966088 | tf_op jit(solution)/shard_map/ppermute | solution.py:61
  167.1 0.6 shard_map.97
  167.7 2.4 %collective-permute-start.15 = (bf16[4,64,640]{2,1,0:T(8,128)(2,1)S(1)}, bf16[4,64,640]{2,1,0:T(8,128)(2,1)S(1)}, u32[]{:S(2)}, u32[]{:S(2)}) collective-permute-start(bf16[4,64,640]{2,1,0:T(8,128)(2,1)S(1)} %shard_map.97), channel_id=1, source_target_pairs={{0,1},{1,0},{2,3},{3,2},{4,5},{5,4},{6,7},{7,6},{8,9},{9,8},{10,11... | collective-permute-start | bytes 983048 | tf_op jit(solution)/shard_map/ppermute | solution.py:61
  170.1 1.2 collective-permute-done.15.refs_4_
  171.4 1.4 shard_map.98
  172.8 0.0 collective-permute-done.19.refs_4_
  172.8 1.7 shard_map.100
  (8 shorter events, 0.0 us)
Async XLA Ops:
  0.7 0.7 copy-start.5
  0.7 0.7 copy-start.4
  1.6 1.1 copy-start.2
  2.7 1.1 copy-start.3
  3.8 2.5 %copy-start = (bf16[64,5120]{1,0:T(8,128)(2,1)S(1)}, bf16[64,5120]{1,0:T(8,128)(2,1)}, u32[]{:S(2)}) copy-start(bf16[64,5120]{1,0:T(8,128)(2,1)} %refs_1_.9) | copy-start | bytes 1966084
  3.8 2.6 %copy-start.1 = (bf16[64,5120]{1,0:T(8,128)(2,1)S(1)}, bf16[64,5120]{1,0:T(8,128)(2,1)}, u32[]{:S(2)}) copy-start(bf16[64,5120]{1,0:T(8,128)(2,1)} %refs_2_.1) | copy-start | bytes 1966084
  4.4 5.0 %collective-permute-start = (bf16[4,144,640]{2,1,0:T(8,128)(2,1)S(1)}, bf16[4,144,640]{2,1,0:T(8,128)(2,1)S(1)}, u32[]{:S(2)}, u32[]{:S(2)}) collective-permute-start(bf16[4,144,640]{2,1,0:T(8,128)(2,1)S(1)} %shard_map.85), channel_id=1, source_target_pairs={{0,1},{1,0},{2,3},{3,2},{4,5},{5,4},{6,7},{7,6},{8,9},{9,8},{10,11... | collective-permute-start | bytes 2211848 | tf_op jit(solution)/shard_map/ppermute | solution.py:61
  6.9 22.0 %collective-permute-start.2 = (bf16[4,128,640]{2,1,0:T(8,128)(2,1)S(1)}, bf16[4,128,640]{2,1,0:T(8,128)(2,1)S(1)}, u32[]{:S(2)}, u32[]{:S(2)}) collective-permute-start(bf16[4,128,640]{2,1,0:T(8,128)(2,1)S(1)} %shard_map.88), channel_id=1, source_target_pairs={{0,1},{1,0},{2,3},{3,2},{4,5},{5,4},{6,7},{7,6},{8,9},{9,8},{10,11... | collective-permute-start | bytes 1966088 | tf_op jit(solution)/shard_map/ppermute | solution.py:61
  10.0 27.5 %collective-permute-start.1 = (bf16[272,640]{1,0:T(8,128)(2,1)S(1)}, bf16[272,640]{1,0:T(8,128)(2,1)S(1)}, u32[]{:S(2)}, u32[]{:S(2)}) collective-permute-start(bf16[272,640]{1,0:T(8,128)(2,1)S(1)} %get-tuple-element.33), channel_id=1, source_target_pairs={{0,2},{1,3},{2,4},{3,5},{4,6},{5,7},{6,0},{7,1},{8,10},{9,11},{10,... | collective-permute-start | bytes 1044488 | tf_op jit(solution)/shard_map/ppermute | solution.py:61
  16.1 61.7 %collective-permute-start.5 = (bf16[272,640]{1,0:T(8,128)(2,1)S(1)}, bf16[272,640]{1,0:T(8,128)(2,1)S(1)}, u32[]{:S(2)}, u32[]{:S(2)}) collective-permute-start(bf16[272,640]{1,0:T(8,128)(2,1)S(1)} %get-tuple-element.36), channel_id=1, source_target_pairs={{0,6},{1,7},{2,0},{3,1},{4,2},{5,3},{6,4},{7,5},{8,14},{9,15},{10,... | collective-permute-start | bytes 1044488 | tf_op jit(solution)/shard_map/ppermute | solution.py:61
  22.9 54.9 %collective-permute-start.6 = (bf16[272,640]{1,0:T(8,128)(2,1)S(1)}, bf16[272,640]{1,0:T(8,128)(2,1)S(1)}, u32[]{:S(2)}, u32[]{:S(2)}) collective-permute-start(bf16[272,640]{1,0:T(8,128)(2,1)S(1)} %get-tuple-element.37), channel_id=1, source_target_pairs={{0,4},{1,5},{2,6},{3,7},{4,0},{5,1},{6,2},{7,3},{8,12},{9,13},{10,... | collective-permute-start | bytes 1044488 | tf_op jit(solution)/shard_map/ppermute | solution.py:61
  29.5 48.3 %collective-permute-start.3 = (bf16[256,640]{1,0:T(8,128)(2,1)S(1)}, bf16[256,640]{1,0:T(8,128)(2,1)S(1)}, u32[]{:S(2)}, u32[]{:S(2)}) collective-permute-start(bf16[256,640]{1,0:T(8,128)(2,1)S(1)} %get-tuple-element.34), channel_id=1, source_target_pairs={{0,2},{1,3},{2,4},{3,5},{4,6},{5,7},{6,0},{7,1},{8,10},{9,11},{10,... | collective-permute-start | bytes 983048 | tf_op jit(solution)/shard_map/ppermute | solution.py:61
  32.6 45.2 %collective-permute-start.4 = (bf16[256,640]{1,0:T(8,128)(2,1)S(1)}, bf16[256,640]{1,0:T(8,128)(2,1)S(1)}, u32[]{:S(2)}, u32[]{:S(2)}) collective-permute-start(bf16[256,640]{1,0:T(8,128)(2,1)S(1)} %get-tuple-element.35), channel_id=1, source_target_pairs={{0,6},{1,7},{2,0},{3,1},{4,2},{5,3},{6,4},{7,5},{8,14},{9,15},{10,... | collective-permute-start | bytes 983048 | tf_op jit(solution)/shard_map/ppermute | solution.py:61
  38.1 47.9 %collective-permute-start.7 = (bf16[544,640]{1,0:T(8,128)(2,1)S(1)}, bf16[544,640]{1,0:T(8,128)(2,1)S(1)}, u32[]{:S(2)}, u32[]{:S(2)}) collective-permute-start(bf16[544,640]{1,0:T(8,128)(2,1)S(1)} %shard_map.87.refs_0_), channel_id=1, source_target_pairs={{0,8},{1,9},{2,10},{3,11},{4,12},{5,13},{6,14},{7,15},{8,16},{9,17... | collective-permute-start | bytes 2088968 | tf_op jit(solution)/shard_map/ppermute | solution.py:61
  78.4 23.0 %collective-permute-start.8 = (bf16[544,640]{1,0:T(8,128)(2,1)S(1)}, bf16[544,640]{1,0:T(8,128)(2,1)S(1)}, u32[]{:S(2)}, u32[]{:S(2)}) collective-permute-start(bf16[544,640]{1,0:T(8,128)(2,1)S(1)} %shard_map.90.refs_1_), channel_id=1, source_target_pairs={{0,8},{1,9},{2,10},{3,11},{4,12},{5,13},{6,14},{7,15},{8,16},{9,17... | collective-permute-start | bytes 2088968 | tf_op jit(solution)/shard_map/ppermute | solution.py:61
  81.0 27.9 %collective-permute-start.9 = (bf16[256,640]{1,0:T(8,128)(2,1)S(1)}, bf16[256,640]{1,0:T(8,128)(2,1)S(1)}, u32[]{:S(2)}, u32[]{:S(2)}) collective-permute-start(bf16[256,640]{1,0:T(8,128)(2,1)S(1)} %get-tuple-element.38), channel_id=1, source_target_pairs={{0,4},{1,5},{2,6},{3,7},{4,0},{5,1},{6,2},{7,3},{8,12},{9,13},{10,... | collective-permute-start | bytes 983048 | tf_op jit(solution)/shard_map/ppermute | solution.py:61
  113.8 14.7 %collective-permute-start.10 = (bf16[256,640]{1,0:T(8,128)(2,1)S(1)}, bf16[256,640]{1,0:T(8,128)(2,1)S(1)}, u32[]{:S(2)}, u32[]{:S(2)}) collective-permute-start(bf16[256,640]{1,0:T(8,128)(2,1)S(1)} %get-tuple-element.48), channel_id=1, source_target_pairs={{8,0},{9,1},{10,2},{11,3},{12,4},{13,5},{14,6},{15,7},{16,8},{17,9... | collective-permute-start | bytes 983048 | tf_op jit(solution)/shard_map/ppermute | solution.py:61
  115.7 18.0 %collective-permute-start.12 = (bf16[256,640]{1,0:T(8,128)(2,1)S(1)}, bf16[256,640]{1,0:T(8,128)(2,1)S(1)}, u32[]{:S(2)}, u32[]{:S(2)}) collective-permute-start(bf16[256,640]{1,0:T(8,128)(2,1)S(1)} %get-tuple-element.52), channel_id=1, source_target_pairs={{8,0},{9,1},{10,2},{11,3},{12,4},{13,5},{14,6},{15,7},{16,8},{17,9... | collective-permute-start | bytes 983048 | tf_op jit(solution)/shard_map/ppermute | solution.py:61
  117.6 23.7 %collective-permute-start.17 = (bf16[256,640]{1,0:T(8,128)(2,1)S(1)}, bf16[256,640]{1,0:T(8,128)(2,1)S(1)}, u32[]{:S(2)}, u32[]{:S(2)}) collective-permute-start(bf16[256,640]{1,0:T(8,128)(2,1)S(1)} %get-tuple-element.57), channel_id=1, source_target_pairs={{4,0},{5,1},{6,2},{7,3},{0,4},{1,5},{2,6},{3,7},{12,8},{13,9},{14,... | collective-permute-start | bytes 983048 | tf_op jit(solution)/shard_map/ppermute | solution.py:61
  121.6 39.5 %collective-permute-start.16 = (bf16[256,640]{1,0:T(8,128)(2,1)S(1)}, bf16[256,640]{1,0:T(8,128)(2,1)S(1)}, u32[]{:S(2)}, u32[]{:S(2)}) collective-permute-start(bf16[256,640]{1,0:T(8,128)(2,1)S(1)} %get-tuple-element.56), channel_id=1, source_target_pairs={{2,0},{3,1},{4,2},{5,3},{6,4},{7,5},{0,6},{1,7},{10,8},{11,9},{12,... | collective-permute-start | bytes 983048 | tf_op jit(solution)/shard_map/ppermute | solution.py:61
  125.1 36.1 %collective-permute-start.18 = (bf16[256,640]{1,0:T(8,128)(2,1)S(1)}, bf16[256,640]{1,0:T(8,128)(2,1)S(1)}, u32[]{:S(2)}, u32[]{:S(2)}) collective-permute-start(bf16[256,640]{1,0:T(8,128)(2,1)S(1)} %get-tuple-element.58), channel_id=1, source_target_pairs={{6,0},{7,1},{0,2},{1,3},{2,4},{3,5},{4,6},{5,7},{14,8},{15,9},{8,1... | collective-permute-start | bytes 983048 | tf_op jit(solution)/shard_map/ppermute | solution.py:61
  129.1 35.5 %collective-permute-start.11 = (bf16[128,640]{1,0:T(8,128)(2,1)S(1)}, bf16[128,640]{1,0:T(8,128)(2,1)S(1)}, u32[]{:S(2)}, u32[]{:S(2)}) collective-permute-start(bf16[128,640]{1,0:T(8,128)(2,1)S(1)} %get-tuple-element.50), channel_id=1, source_target_pairs={{2,0},{3,1},{4,2},{5,3},{6,4},{7,5},{0,6},{1,7},{10,8},{11,9},{12,... | collective-permute-start | bytes 491528 | tf_op jit(solution)/shard_map/ppermute | solution.py:61
  134.4 30.2 %collective-permute-start.13 = (bf16[128,640]{1,0:T(8,128)(2,1)S(1)}, bf16[128,640]{1,0:T(8,128)(2,1)S(1)}, u32[]{:S(2)}, u32[]{:S(2)}) collective-permute-start(bf16[128,640]{1,0:T(8,128)(2,1)S(1)} %get-tuple-element.53), channel_id=1, source_target_pairs={{4,0},{5,1},{6,2},{7,3},{0,4},{1,5},{2,6},{3,7},{12,8},{13,9},{14,... | collective-permute-start | bytes 491528 | tf_op jit(solution)/shard_map/ppermute | solution.py:61
  141.3 23.3 %collective-permute-start.14 = (bf16[128,640]{1,0:T(8,128)(2,1)S(1)}, bf16[128,640]{1,0:T(8,128)(2,1)S(1)}, u32[]{:S(2)}, u32[]{:S(2)}) collective-permute-start(bf16[128,640]{1,0:T(8,128)(2,1)S(1)} %get-tuple-element.54), channel_id=1, source_target_pairs={{6,0},{7,1},{0,2},{1,3},{2,4},{3,5},{4,6},{5,7},{14,8},{15,9},{8,1... | collective-permute-start | bytes 491528 | tf_op jit(solution)/shard_map/ppermute | solution.py:61
  165.2 7.6 %collective-permute-start.19 = (bf16[4,128,640]{2,1,0:T(8,128)(2,1)S(1)}, bf16[4,128,640]{2,1,0:T(8,128)(2,1)S(1)}, u32[]{:S(2)}, u32[]{:S(2)}) collective-permute-start(bf16[4,128,640]{2,1,0:T(8,128)(2,1)S(1)} %shard_map.99), channel_id=1, source_target_pairs={{0,1},{1,0},{2,3},{3,2},{4,5},{5,4},{6,7},{7,6},{8,9},{9,8},{10,11... | collective-permute-start | bytes 1966088 | tf_op jit(solution)/shard_map/ppermute | solution.py:61
  167.7 3.6 %collective-permute-start.15 = (bf16[4,64,640]{2,1,0:T(8,128)(2,1)S(1)}, bf16[4,64,640]{2,1,0:T(8,128)(2,1)S(1)}, u32[]{:S(2)}, u32[]{:S(2)}) collective-permute-start(bf16[4,64,640]{2,1,0:T(8,128)(2,1)S(1)} %shard_map.97), channel_id=1, source_target_pairs={{0,1},{1,0},{2,3},{3,2},{4,5},{5,4},{6,7},{7,6},{8,9},{9,8},{10,11... | collective-permute-start | bytes 983048 | tf_op jit(solution)/shard_map/ppermute | solution.py:61

commit v3 on v2

--- a/solution.py
+++ b/solution.py
@@ -12,7 +12,7 @@
 AXES = ("blk", "uly")
 CHIPS = 4
 RING = 8
-PAD = 16
+PAD = 8
 
 
 def shift(b, core):
@@ -32,19 +32,6 @@
             chip = (chip + shift(b, core) - shift(after, core)) % CHIPS
             pairs.append((b * 8 + u, after * 8 + 2 * chip + core))
     return pairs
-
-
-def hop_pairs(blocks):
-    pairs = []
-    for s, t in next_pairs(blocks):
-        b = s // 8
-        pairs.append((s, (b ^ RING) * 8 + t % 8 if b % RING == RING - 1 else s))
-    return pairs
-
-
-def after_hop_pairs(blocks):
-    onward = dict(next_pairs(blocks))
-    return [(t, onward[s]) for s, t in hop_pairs(blocks)]
 
 
 def back(pairs):
@@ -288,7 +275,6 @@
     there = [gather_pairs(blocks, d) for d in range(CHIPS)]
     home = [back(pairs) for pairs in there]
     onward = next_pairs(blocks)
-    hop, after_hop = hop_pairs(blocks), after_hop_pairs(blocks)
 
     other = moved(other_core_parts(query_rows, out_grad, stats, place), cores)
     other_keys = moved(other_core_parts(key_rows, value_rows, None, place), cores)

time: 178 us -> 180 us (1.011)
  the two profiles are of different devices: /device:TPU:6 before, /device:TPU:77 now
where the time goes in v3:
time: 180 us; the launch traced here: 179 us
  starting transfers between devices  87.4 us (49%)
  waiting for transfers between devices  62.7 us (35%)
  Pallas kernels  24.9 us (14%)
  local copies, waits for them, and re-layouts  2.9 us (2%)
    ppermute x20, starting transfers between devices, moved(): return lax.ppermute(value, AXES, pairs)  87.4 us
    ppermute x20, waiting for transfers between devices, moved(): return lax.ppermute(value, AXES, pairs)  62.7 us
    pallas_call x3, Pallas kernels, grads(): pl.pallas_call(kernel, grid=(heads,), in_specs=[block(2 * size)] * len(qu...  15.1 us
    pallas_call x13, Pallas kernels, call(): pl.pallas_call(body, out_shape=out_shape, in_specs=[pl.BlockSpec(memory_s...  9.81 us
  transfers between devices with their start and end apart: 20, of which 9 were waited for; matrix products, arithmetic and copies ran while one was open for 0% of the time, Pallas kernels for 10%

profile of v3, /device:TPU:77, one launch (start us, length us, event | category | flops | bytes accessed | tf_op | source)
XLA Modules:
  0.0 179.1 jit_solution(7493317818444107768)
XLA Ops:
  0.7 0.0 copy-start.5
  0.7 0.0 copy-start.4
  0.7 0.7 copy-done.5
  1.4 0.0 copy-done.4
  1.4 0.1 pad_maximum_fusion
  1.5 0.1 pad_add_fusion.place_ref
  1.6 1.1 copy-done.2
  2.7 1.1 copy-done.3
  3.8 0.6 shard_map.85
  4.4 2.6 %collective-permute-start = (bf16[4,136,640]{2,1,0:T(8,128)(2,1)S(1)}, bf16[4,136,640]{2,1,0:T(8,128)(2,1)S(1)}, u32[]{:S(2)}, u32[]{:S(2)}) collective-permute-start(bf16[4,136,640]{2,1,0:T(8,128)(2,1)S(1)} %shard_map.85), channel_id=1, source_target_pairs={{0,1},{1,0},{2,3},{3,2},{4,5},{5,4},{6,7},{7,6},{8,9},{9,8},{10,11... | collective-permute-start | bytes 2088968 | tf_op jit(solution)/shard_map/ppermute | solution.py:48
  7.0 0.6 shard_map.88
  7.6 1.9 %collective-permute-start.2 = (bf16[4,128,640]{2,1,0:T(8,128)(2,1)S(1)}, bf16[4,128,640]{2,1,0:T(8,128)(2,1)S(1)}, u32[]{:S(2)}, u32[]{:S(2)}) collective-permute-start(bf16[4,128,640]{2,1,0:T(8,128)(2,1)S(1)} %shard_map.88), channel_id=1, source_target_pairs={{0,1},{1,0},{2,3},{3,2},{4,5},{5,4},{6,7},{7,6},{8,9},{9,8},{10,11... | collective-permute-start | bytes 1966088 | tf_op jit(solution)/shard_map/ppermute | solution.py:48
  9.5 0.0 collective-permute-done.refs_3_
  9.5 0.7 shard_map.86
  10.2 5.8 %collective-permute-start.1 = (bf16[264,640]{1,0:T(8,128)(2,1)S(1)}, bf16[264,640]{1,0:T(8,128)(2,1)S(1)}, u32[]{:S(2)}, u32[]{:S(2)}) collective-permute-start(bf16[264,640]{1,0:T(8,128)(2,1)S(1)} %get-tuple-element.33), channel_id=1, source_target_pairs={{0,2},{1,3},{2,4},{3,5},{4,6},{5,7},{6,0},{7,1},{8,10},{9,11},{10,... | collective-permute-start | bytes 1013768 | tf_op jit(solution)/shard_map/ppermute | solution.py:48
  16.0 5.9 %collective-permute-start.5 = (bf16[264,640]{1,0:T(8,128)(2,1)S(1)}, bf16[264,640]{1,0:T(8,128)(2,1)S(1)}, u32[]{:S(2)}, u32[]{:S(2)}) collective-permute-start(bf16[264,640]{1,0:T(8,128)(2,1)S(1)} %get-tuple-element.36), channel_id=1, source_target_pairs={{0,6},{1,7},{2,0},{3,1},{4,2},{5,3},{6,4},{7,5},{8,14},{9,15},{10,... | collective-permute-start | bytes 1013768 | tf_op jit(solution)/shard_map/ppermute | solution.py:48
  21.9 5.5 %collective-permute-start.6 = (bf16[264,640]{1,0:T(8,128)(2,1)S(1)}, bf16[264,640]{1,0:T(8,128)(2,1)S(1)}, u32[]{:S(2)}, u32[]{:S(2)}) collective-permute-start(bf16[264,640]{1,0:T(8,128)(2,1)S(1)} %get-tuple-element.37), channel_id=1, source_target_pairs={{0,4},{1,5},{2,6},{3,7},{4,0},{5,1},{6,2},{7,3},{8,12},{9,13},{10,... | collective-permute-start | bytes 1013768 | tf_op jit(solution)/shard_map/ppermute | solution.py:48
  27.4 0.0 collective-permute-done.2.refs_2_.refs_3_
  27.4 0.6 shard_map.89
  28.0 2.8 %collective-permute-start.3 = (bf16[256,640]{1,0:T(8,128)(2,1)S(1)}, bf16[256,640]{1,0:T(8,128)(2,1)S(1)}, u32[]{:S(2)}, u32[]{:S(2)}) collective-permute-start(bf16[256,640]{1,0:T(8,128)(2,1)S(1)} %get-tuple-element.34), channel_id=1, source_target_pairs={{0,2},{1,3},{2,4},{3,5},{4,6},{5,7},{6,0},{7,1},{8,10},{9,11},{10,... | collective-permute-start | bytes 983048 | tf_op jit(solution)/shard_map/ppermute | solution.py:48
  30.8 4.6 %collective-permute-start.4 = (bf16[256,640]{1,0:T(8,128)(2,1)S(1)}, bf16[256,640]{1,0:T(8,128)(2,1)S(1)}, u32[]{:S(2)}, u32[]{:S(2)}) collective-permute-start(bf16[256,640]{1,0:T(8,128)(2,1)S(1)} %get-tuple-element.35), channel_id=1, source_target_pairs={{0,6},{1,7},{2,0},{3,1},{4,2},{5,3},{6,4},{7,5},{8,14},{9,15},{10,... | collective-permute-start | bytes 983048 | tf_op jit(solution)/shard_map/ppermute | solution.py:48
  35.4 1.0 collective-permute-done.1.refs_1_.refs_0_
  36.4 0.6 shard_map.87.refs_0_
  37.0 3.2 %collective-permute-start.7 = (bf16[528,640]{1,0:T(8,128)(2,1)S(1)}, bf16[528,640]{1,0:T(8,128)(2,1)S(1)}, u32[]{:S(2)}, u32[]{:S(2)}) collective-permute-start(bf16[528,640]{1,0:T(8,128)(2,1)S(1)} %shard_map.87.refs_0_), channel_id=1, source_target_pairs={{0,8},{1,9},{2,10},{3,11},{4,12},{5,13},{6,14},{7,15},{8,16},{9,17... | collective-permute-start | bytes 2027528 | tf_op jit(solution)/shard_map/ppermute | solution.py:48
  40.2 5.4 %collective-permute-done.3.refs_0_.refs_4_.refs_2_ = bf16[256,640]{1,0:T(8,128)(2,1)S(1)} collective-permute-done((bf16[256,640]{1,0:T(8,128)(2,1)S(1)}, bf16[256,640]{1,0:T(8,128)(2,1)S(1)}, u32[]{:S(2)}, u32[]{:S(2)}) %collective-permute-start.3) | collective-permute-done | bytes 327712 | tf_op jit(solution)/shard_map/ppermute | solution.py:48
  45.6 19.9 %collective-permute-done.4.refs_1_.refs_5_.refs_3_ = bf16[256,640]{1,0:T(8,128)(2,1)S(1)} collective-permute-done((bf16[256,640]{1,0:T(8,128)(2,1)S(1)}, bf16[256,640]{1,0:T(8,128)(2,1)S(1)}, u32[]{:S(2)}, u32[]{:S(2)}) %collective-permute-start.4) | collective-permute-done | bytes 327712 | tf_op jit(solution)/shard_map/ppermute | solution.py:48
  65.5 0.0 collective-permute-done.5.refs_2_
  65.5 0.0 collective-permute-done.6.refs_3_
  65.5 0.6 shard_map.90.refs_1_
  66.2 3.2 %collective-permute-start.8 = (bf16[528,640]{1,0:T(8,128)(2,1)S(1)}, bf16[528,640]{1,0:T(8,128)(2,1)S(1)}, u32[]{:S(2)}, u32[]{:S(2)}) collective-permute-start(bf16[528,640]{1,0:T(8,128)(2,1)S(1)} %shard_map.90.refs_1_), channel_id=1, source_target_pairs={{0,8},{1,9},{2,10},{3,11},{4,12},{5,13},{6,14},{7,15},{8,16},{9,17... | collective-permute-start | bytes 2027528 | tf_op jit(solution)/shard_map/ppermute | solution.py:48
  69.4 0.6 shard_map.91
  70.0 7.0 %collective-permute-start.9 = (bf16[256,640]{1,0:T(8,128)(2,1)S(1)}, bf16[256,640]{1,0:T(8,128)(2,1)S(1)}, u32[]{:S(2)}, u32[]{:S(2)}) collective-permute-start(bf16[256,640]{1,0:T(8,128)(2,1)S(1)} %get-tuple-element.38), channel_id=1, source_target_pairs={{0,4},{1,5},{2,6},{3,7},{4,0},{5,1},{6,2},{7,3},{8,12},{9,13},{10,... | collective-permute-start | bytes 983048 | tf_op jit(solution)/shard_map/ppermute | solution.py:48
  76.9 0.0 collective-permute-done.7.refs_2_
  77.0 6.8 %shard_map.92 = (f32[256,640]{1,0:T(8,128)S(1)}, f32[256,640]{1,0:T(8,128)S(1)}, f32[256,640]{1,0:T(8,128)S(1)}, f32[256,640]{1,0:T(8,128)S(1)}, f32[256,640]{1,0:T(8,128)S(1)}, /*index=5*/f32[256,640]{1,0:T(8,128)S(1)}) custom-call(bf16[528,640]{1,0:T(8,128)(2,1)S(1)} %shard_map.87.refs_0_, bf16[528,640]{1,0:T(8,128)(2,1)S(1)} %shard_map.90.refs_1_, ...), custom_call_target="tpu_custom_call" | custom-call | flops 1887436800 | bytes 8388608 | tf_op jit(solution)/shard_map/pallas_call | solution.py:209
  83.7 8.3 %collective-permute-done.8.refs_0_.refs_3_ = bf16[528,640]{1,0:T(8,128)(2,1)S(1)} collective-permute-done((bf16[528,640]{1,0:T(8,128)(2,1)S(1)}, bf16[528,640]{1,0:T(8,128)(2,1)S(1)}, u32[]{:S(2)}, u32[]{:S(2)}) %collective-permute-start.8) | collective-permute-done | bytes 675872 | tf_op jit(solution)/shard_map/ppermute | solution.py:48
  92.0 3.4 %shard_map.93 = (f32[256,640]{1,0:T(8,128)S(1)}, bf16[256,640]{1,0:T(8,128)(2,1)S(1)}, bf16[256,640]{1,0:T(8,128)(2,1)S(1)}, bf16[256,640]{1,0:T(8,128)(2,1)S(1)}) custom-call(bf16[528,640]{1,0:T(8,128)(2,1)S(1)} %collective-permute-done.8.refs_0_.refs_3_, bf16[256,640]{1,0:T(8,128)(2,1)S(1)} %get-tuple-element.39.refs_3_.refs_1_, ...), custom_call_target="tpu_custom_call" | custom-call | flops 629145600 | bytes 8388608 | tf_op jit(solution)/shard_map/pallas_call | solution.py:209
  95.4 0.0 collective-permute-done.9.refs_4_
  95.4 4.9 %shard_map.94 = (f32[256,640]{1,0:T(8,128)S(1)}, f32[256,640]{1,0:T(8,128)S(1)}, bf16[256,640]{1,0:T(8,128)(2,1)S(1)}, bf16[256,640]{1,0:T(8,128)(2,1)S(1)}, bf16[256,640]{1,0:T(8,128)(2,1)S(1)}) custom-call(bf16[528,640]{1,0:T(8,128)(2,1)S(1)} %shard_map.87.refs_0_, bf16[528,640]{1,0:T(8,128)(2,1)S(1)} %shard_map.90.refs_1_, ...), custom_call_target="tpu_custom_call" | custom-call | flops 838860800 | bytes 8388608 | tf_op jit(solution)/shard_map/pallas_call | solution.py:209
  100.3 16.8 %collective-permute-start.10 = (bf16[256,640]{1,0:T(8,128)(2,1)S(1)}, bf16[256,640]{1,0:T(8,128)(2,1)S(1)}, u32[]{:S(2)}, u32[]{:S(2)}) collective-permute-start(bf16[256,640]{1,0:T(8,128)(2,1)S(1)} %get-tuple-element.48), channel_id=1, source_target_pairs={{8,0},{9,1},{10,2},{11,3},{12,4},{13,5},{14,6},{15,7},{16,8},{17,9... | collective-permute-start | bytes 983048 | tf_op jit(solution)/shard_map/ppermute | solution.py:48
  117.2 1.9 %collective-permute-start.12 = (bf16[256,640]{1,0:T(8,128)(2,1)S(1)}, bf16[256,640]{1,0:T(8,128)(2,1)S(1)}, u32[]{:S(2)}, u32[]{:S(2)}) collective-permute-start(bf16[256,640]{1,0:T(8,128)(2,1)S(1)} %get-tuple-element.52), channel_id=1, source_target_pairs={{8,0},{9,1},{10,2},{11,3},{12,4},{13,5},{14,6},{15,7},{16,8},{17,9... | collective-permute-start | bytes 983048 | tf_op jit(solution)/shard_map/ppermute | solution.py:48
  119.1 6.8 %collective-permute-start.17 = (bf16[256,640]{1,0:T(8,128)(2,1)S(1)}, bf16[256,640]{1,0:T(8,128)(2,1)S(1)}, u32[]{:S(2)}, u32[]{:S(2)}) collective-permute-start(bf16[256,640]{1,0:T(8,128)(2,1)S(1)} %get-tuple-element.57), channel_id=1, source_target_pairs={{4,0},{5,1},{6,2},{7,3},{0,4},{1,5},{2,6},{3,7},{12,8},{13,9},{14,... | collective-permute-start | bytes 983048 | tf_op jit(solution)/shard_map/ppermute | solution.py:48
  125.8 1.9 %collective-permute-start.16 = (bf16[256,640]{1,0:T(8,128)(2,1)S(1)}, bf16[256,640]{1,0:T(8,128)(2,1)S(1)}, u32[]{:S(2)}, u32[]{:S(2)}) collective-permute-start(bf16[256,640]{1,0:T(8,128)(2,1)S(1)} %get-tuple-element.56), channel_id=1, source_target_pairs={{2,0},{3,1},{4,2},{5,3},{6,4},{7,5},{0,6},{1,7},{10,8},{11,9},{12,... | collective-permute-start | bytes 983048 | tf_op jit(solution)/shard_map/ppermute | solution.py:48
  127.8 4.3 %collective-permute-start.18 = (bf16[256,640]{1,0:T(8,128)(2,1)S(1)}, bf16[256,640]{1,0:T(8,128)(2,1)S(1)}, u32[]{:S(2)}, u32[]{:S(2)}) collective-permute-start(bf16[256,640]{1,0:T(8,128)(2,1)S(1)} %get-tuple-element.58), channel_id=1, source_target_pairs={{6,0},{7,1},{0,2},{1,3},{2,4},{3,5},{4,6},{5,7},{14,8},{15,9},{8,1... | collective-permute-start | bytes 983048 | tf_op jit(solution)/shard_map/ppermute | solution.py:48
  132.0 0.0 collective-permute-done.10.refs_1_
  132.1 0.6 shard_map.95
  132.7 3.1 %collective-permute-start.11 = (bf16[128,640]{1,0:T(8,128)(2,1)S(1)}, bf16[128,640]{1,0:T(8,128)(2,1)S(1)}, u32[]{:S(2)}, u32[]{:S(2)}) collective-permute-start(bf16[128,640]{1,0:T(8,128)(2,1)S(1)} %get-tuple-element.50), channel_id=1, source_target_pairs={{2,0},{3,1},{4,2},{5,3},{6,4},{7,5},{0,6},{1,7},{10,8},{11,9},{12,... | collective-permute-start | bytes 491528 | tf_op jit(solution)/shard_map/ppermute | solution.py:48
  135.8 0.0 collective-permute-done.12.refs_1_
  135.8 0.6 shard_map.96
  136.5 4.0 %collective-permute-start.13 = (bf16[128,640]{1,0:T(8,128)(2,1)S(1)}, bf16[128,640]{1,0:T(8,128)(2,1)S(1)}, u32[]{:S(2)}, u32[]{:S(2)}) collective-permute-start(bf16[128,640]{1,0:T(8,128)(2,1)S(1)} %get-tuple-element.53), channel_id=1, source_target_pairs={{4,0},{5,1},{6,2},{7,3},{0,4},{1,5},{2,6},{3,7},{12,8},{13,9},{14,... | collective-permute-start | bytes 491528 | tf_op jit(solution)/shard_map/ppermute | solution.py:48
  140.5 2.7 %collective-permute-done.17.refs_5_.refs_2_ = bf16[256,640]{1,0:T(8,128)(2,1)S(1)} collective-permute-done((bf16[256,640]{1,0:T(8,128)(2,1)S(1)}, bf16[256,640]{1,0:T(8,128)(2,1)S(1)}, u32[]{:S(2)}, u32[]{:S(2)}) %collective-permute-start.17) | collective-permute-done | bytes 327712 | tf_op jit(solution)/shard_map/ppermute | solution.py:48
  143.2 1.9 %collective-permute-start.14 = (bf16[128,640]{1,0:T(8,128)(2,1)S(1)}, bf16[128,640]{1,0:T(8,128)(2,1)S(1)}, u32[]{:S(2)}, u32[]{:S(2)}) collective-permute-start(bf16[128,640]{1,0:T(8,128)(2,1)S(1)} %get-tuple-element.54), channel_id=1, source_target_pairs={{6,0},{7,1},{0,2},{1,3},{2,4},{3,5},{4,6},{5,7},{14,8},{15,9},{8,1... | collective-permute-start | bytes 491528 | tf_op jit(solution)/shard_map/ppermute | solution.py:48
  145.1 0.9 collective-permute-done.16.refs_4_.refs_1_
  146.0 13.1 %collective-permute-done.18.refs_6_.refs_3_ = bf16[256,640]{1,0:T(8,128)(2,1)S(1)} collective-permute-done((bf16[256,640]{1,0:T(8,128)(2,1)S(1)}, bf16[256,640]{1,0:T(8,128)(2,1)S(1)}, u32[]{:S(2)}, u32[]{:S(2)}) %collective-permute-start.18) | collective-permute-done | bytes 327712 | tf_op jit(solution)/shard_map/ppermute | solution.py:48
  159.1 0.0 collective-permute-done.11.refs_1_.refs_0_
  159.1 9.7 %collective-permute-done.13.refs_2_.refs_1_ = bf16[128,640]{1,0:T(8,128)(2,1)S(1)} collective-permute-done((bf16[128,640]{1,0:T(8,128)(2,1)S(1)}, bf16[128,640]{1,0:T(8,128)(2,1)S(1)}, u32[]{:S(2)}, u32[]{:S(2)}) %collective-permute-start.13) | collective-permute-done | bytes 163872 | tf_op jit(solution)/shard_map/ppermute | solution.py:48
  168.8 0.0 collective-permute-done.14.refs_3_.refs_2_
  168.8 0.6 shard_map.99
  169.4 2.4 %collective-permute-start.19 = (bf16[4,128,640]{2,1,0:T(8,128)(2,1)S(1)}, bf16[4,128,640]{2,1,0:T(8,128)(2,1)S(1)}, u32[]{:S(2)}, u32[]{:S(2)}) collective-permute-start(bf16[4,128,640]{2,1,0:T(8,128)(2,1)S(1)} %shard_map.99), channel_id=1, source_target_pairs={{0,1},{1,0},{2,3},{3,2},{4,5},{5,4},{6,7},{7,6},{8,9},{9,8},{10,11... | collective-permute-start | bytes 1966088 | tf_op jit(solution)/shard_map/ppermute | solution.py:48
  171.8 0.6 shard_map.97
  172.4 1.9 %collective-permute-start.15 = (bf16[4,64,640]{2,1,0:T(8,128)(2,1)S(1)}, bf16[4,64,640]{2,1,0:T(8,128)(2,1)S(1)}, u32[]{:S(2)}, u32[]{:S(2)}) collective-permute-start(bf16[4,64,640]{2,1,0:T(8,128)(2,1)S(1)} %shard_map.97), channel_id=1, source_target_pairs={{0,1},{1,0},{2,3},{3,2},{4,5},{5,4},{6,7},{7,6},{8,9},{9,8},{10,11... | collective-permute-start | bytes 983048 | tf_op jit(solution)/shard_map/ppermute | solution.py:48
  174.3 1.6 collective-permute-done.15.refs_4_
  175.9 1.4 shard_map.98
  177.4 0.0 collective-permute-done.19.refs_4_
  177.4 1.7 shard_map.100
  (8 shorter events, 0.0 us)
Async XLA Ops:
  0.7 0.7 copy-start.5
  0.7 0.7 copy-start.4
  1.6 1.1 copy-start.2
  2.7 1.1 copy-start.3
  3.8 3.2 %copy-start = (bf16[64,5120]{1,0:T(8,128)(2,1)S(1)}, bf16[64,5120]{1,0:T(8,128)(2,1)}, u32[]{:S(2)}) copy-start(bf16[64,5120]{1,0:T(8,128)(2,1)} %refs_1_.9) | copy-start | bytes 1966084
  3.8 3.2 %copy-start.1 = (bf16[64,5120]{1,0:T(8,128)(2,1)S(1)}, bf16[64,5120]{1,0:T(8,128)(2,1)}, u32[]{:S(2)}) copy-start(bf16[64,5120]{1,0:T(8,128)(2,1)} %refs_2_.1) | copy-start | bytes 1966084
  4.4 5.2 %collective-permute-start = (bf16[4,136,640]{2,1,0:T(8,128)(2,1)S(1)}, bf16[4,136,640]{2,1,0:T(8,128)(2,1)S(1)}, u32[]{:S(2)}, u32[]{:S(2)}) collective-permute-start(bf16[4,136,640]{2,1,0:T(8,128)(2,1)S(1)} %shard_map.85), channel_id=1, source_target_pairs={{0,1},{1,0},{2,3},{3,2},{4,5},{5,4},{6,7},{7,6},{8,9},{9,8},{10,11... | collective-permute-start | bytes 2088968 | tf_op jit(solution)/shard_map/ppermute | solution.py:48
  7.6 19.8 %collective-permute-start.2 = (bf16[4,128,640]{2,1,0:T(8,128)(2,1)S(1)}, bf16[4,128,640]{2,1,0:T(8,128)(2,1)S(1)}, u32[]{:S(2)}, u32[]{:S(2)}) collective-permute-start(bf16[4,128,640]{2,1,0:T(8,128)(2,1)S(1)} %shard_map.88), channel_id=1, source_target_pairs={{0,1},{1,0},{2,3},{3,2},{4,5},{5,4},{6,7},{7,6},{8,9},{9,8},{10,11... | collective-permute-start | bytes 1966088 | tf_op jit(solution)/shard_map/ppermute | solution.py:48
  10.2 26.2 %collective-permute-start.1 = (bf16[264,640]{1,0:T(8,128)(2,1)S(1)}, bf16[264,640]{1,0:T(8,128)(2,1)S(1)}, u32[]{:S(2)}, u32[]{:S(2)}) collective-permute-start(bf16[264,640]{1,0:T(8,128)(2,1)S(1)} %get-tuple-element.33), channel_id=1, source_target_pairs={{0,2},{1,3},{2,4},{3,5},{4,6},{5,7},{6,0},{7,1},{8,10},{9,11},{10,... | collective-permute-start | bytes 1013768 | tf_op jit(solution)/shard_map/ppermute | solution.py:48
  16.0 49.5 %collective-permute-start.5 = (bf16[264,640]{1,0:T(8,128)(2,1)S(1)}, bf16[264,640]{1,0:T(8,128)(2,1)S(1)}, u32[]{:S(2)}, u32[]{:S(2)}) collective-permute-start(bf16[264,640]{1,0:T(8,128)(2,1)S(1)} %get-tuple-element.36), channel_id=1, source_target_pairs={{0,6},{1,7},{2,0},{3,1},{4,2},{5,3},{6,4},{7,5},{8,14},{9,15},{10,... | collective-permute-start | bytes 1013768 | tf_op jit(solution)/shard_map/ppermute | solution.py:48
  21.9 43.6 %collective-permute-start.6 = (bf16[264,640]{1,0:T(8,128)(2,1)S(1)}, bf16[264,640]{1,0:T(8,128)(2,1)S(1)}, u32[]{:S(2)}, u32[]{:S(2)}) collective-permute-start(bf16[264,640]{1,0:T(8,128)(2,1)S(1)} %get-tuple-element.37), channel_id=1, source_target_pairs={{0,4},{1,5},{2,6},{3,7},{4,0},{5,1},{6,2},{7,3},{8,12},{9,13},{10,... | collective-permute-start | bytes 1013768 | tf_op jit(solution)/shard_map/ppermute | solution.py:48
  28.0 17.6 %collective-permute-start.3 = (bf16[256,640]{1,0:T(8,128)(2,1)S(1)}, bf16[256,640]{1,0:T(8,128)(2,1)S(1)}, u32[]{:S(2)}, u32[]{:S(2)}) collective-permute-start(bf16[256,640]{1,0:T(8,128)(2,1)S(1)} %get-tuple-element.34), channel_id=1, source_target_pairs={{0,2},{1,3},{2,4},{3,5},{4,6},{5,7},{6,0},{7,1},{8,10},{9,11},{10,... | collective-permute-start | bytes 983048 | tf_op jit(solution)/shard_map/ppermute | solution.py:48
  30.8 34.8 %collective-permute-start.4 = (bf16[256,640]{1,0:T(8,128)(2,1)S(1)}, bf16[256,640]{1,0:T(8,128)(2,1)S(1)}, u32[]{:S(2)}, u32[]{:S(2)}) collective-permute-start(bf16[256,640]{1,0:T(8,128)(2,1)S(1)} %get-tuple-element.35), channel_id=1, source_target_pairs={{0,6},{1,7},{2,0},{3,1},{4,2},{5,3},{6,4},{7,5},{8,14},{9,15},{10,... | collective-permute-start | bytes 983048 | tf_op jit(solution)/shard_map/ppermute | solution.py:48
  37.0 40.0 %collective-permute-start.7 = (bf16[528,640]{1,0:T(8,128)(2,1)S(1)}, bf16[528,640]{1,0:T(8,128)(2,1)S(1)}, u32[]{:S(2)}, u32[]{:S(2)}) collective-permute-start(bf16[528,640]{1,0:T(8,128)(2,1)S(1)} %shard_map.87.refs_0_), channel_id=1, source_target_pairs={{0,8},{1,9},{2,10},{3,11},{4,12},{5,13},{6,14},{7,15},{8,16},{9,17... | collective-permute-start | bytes 2027528 | tf_op jit(solution)/shard_map/ppermute | solution.py:48
  66.2 25.9 %collective-permute-start.8 = (bf16[528,640]{1,0:T(8,128)(2,1)S(1)}, bf16[528,640]{1,0:T(8,128)(2,1)S(1)}, u32[]{:S(2)}, u32[]{:S(2)}) collective-permute-start(bf16[528,640]{1,0:T(8,128)(2,1)S(1)} %shard_map.90.refs_1_), channel_id=1, source_target_pairs={{0,8},{1,9},{2,10},{3,11},{4,12},{5,13},{6,14},{7,15},{8,16},{9,17... | collective-permute-start | bytes 2027528 | tf_op jit(solution)/shard_map/ppermute | solution.py:48
  70.0 25.4 %collective-permute-start.9 = (bf16[256,640]{1,0:T(8,128)(2,1)S(1)}, bf16[256,640]{1,0:T(8,128)(2,1)S(1)}, u32[]{:S(2)}, u32[]{:S(2)}) collective-permute-start(bf16[256,640]{1,0:T(8,128)(2,1)S(1)} %get-tuple-element.38), channel_id=1, source_target_pairs={{0,4},{1,5},{2,6},{3,7},{4,0},{5,1},{6,2},{7,3},{8,12},{9,13},{10,... | collective-permute-start | bytes 983048 | tf_op jit(solution)/shard_map/ppermute | solution.py:48
  100.3 31.7 %collective-permute-start.10 = (bf16[256,640]{1,0:T(8,128)(2,1)S(1)}, bf16[256,640]{1,0:T(8,128)(2,1)S(1)}, u32[]{:S(2)}, u32[]{:S(2)}) collective-permute-start(bf16[256,640]{1,0:T(8,128)(2,1)S(1)} %get-tuple-element.48), channel_id=1, source_target_pairs={{8,0},{9,1},{10,2},{11,3},{12,4},{13,5},{14,6},{15,7},{16,8},{17,9... | collective-permute-start | bytes 983048 | tf_op jit(solution)/shard_map/ppermute | solution.py:48
  117.2 18.7 %collective-permute-start.12 = (bf16[256,640]{1,0:T(8,128)(2,1)S(1)}, bf16[256,640]{1,0:T(8,128)(2,1)S(1)}, u32[]{:S(2)}, u32[]{:S(2)}) collective-permute-start(bf16[256,640]{1,0:T(8,128)(2,1)S(1)} %get-tuple-element.52), channel_id=1, source_target_pairs={{8,0},{9,1},{10,2},{11,3},{12,4},{13,5},{14,6},{15,7},{16,8},{17,9... | collective-permute-start | bytes 983048 | tf_op jit(solution)/shard_map/ppermute | solution.py:48
  119.1 24.1 %collective-permute-start.17 = (bf16[256,640]{1,0:T(8,128)(2,1)S(1)}, bf16[256,640]{1,0:T(8,128)(2,1)S(1)}, u32[]{:S(2)}, u32[]{:S(2)}) collective-permute-start(bf16[256,640]{1,0:T(8,128)(2,1)S(1)} %get-tuple-element.57), channel_id=1, source_target_pairs={{4,0},{5,1},{6,2},{7,3},{0,4},{1,5},{2,6},{3,7},{12,8},{13,9},{14,... | collective-permute-start | bytes 983048 | tf_op jit(solution)/shard_map/ppermute | solution.py:48
  125.8 20.1 %collective-permute-start.16 = (bf16[256,640]{1,0:T(8,128)(2,1)S(1)}, bf16[256,640]{1,0:T(8,128)(2,1)S(1)}, u32[]{:S(2)}, u32[]{:S(2)}) collective-permute-start(bf16[256,640]{1,0:T(8,128)(2,1)S(1)} %get-tuple-element.56), channel_id=1, source_target_pairs={{2,0},{3,1},{4,2},{5,3},{6,4},{7,5},{0,6},{1,7},{10,8},{11,9},{12,... | collective-permute-start | bytes 983048 | tf_op jit(solution)/shard_map/ppermute | solution.py:48
  127.8 31.3 %collective-permute-start.18 = (bf16[256,640]{1,0:T(8,128)(2,1)S(1)}, bf16[256,640]{1,0:T(8,128)(2,1)S(1)}, u32[]{:S(2)}, u32[]{:S(2)}) collective-permute-start(bf16[256,640]{1,0:T(8,128)(2,1)S(1)} %get-tuple-element.58), channel_id=1, source_target_pairs={{6,0},{7,1},{0,2},{1,3},{2,4},{3,5},{4,6},{5,7},{14,8},{15,9},{8,1... | collective-permute-start | bytes 983048 | tf_op jit(solution)/shard_map/ppermute | solution.py:48
  132.7 26.4 %collective-permute-start.11 = (bf16[128,640]{1,0:T(8,128)(2,1)S(1)}, bf16[128,640]{1,0:T(8,128)(2,1)S(1)}, u32[]{:S(2)}, u32[]{:S(2)}) collective-permute-start(bf16[128,640]{1,0:T(8,128)(2,1)S(1)} %get-tuple-element.50), channel_id=1, source_target_pairs={{2,0},{3,1},{4,2},{5,3},{6,4},{7,5},{0,6},{1,7},{10,8},{11,9},{12,... | collective-permute-start | bytes 491528 | tf_op jit(solution)/shard_map/ppermute | solution.py:48
  136.5 32.4 %collective-permute-start.13 = (bf16[128,640]{1,0:T(8,128)(2,1)S(1)}, bf16[128,640]{1,0:T(8,128)(2,1)S(1)}, u32[]{:S(2)}, u32[]{:S(2)}) collective-permute-start(bf16[128,640]{1,0:T(8,128)(2,1)S(1)} %get-tuple-element.53), channel_id=1, source_target_pairs={{4,0},{5,1},{6,2},{7,3},{0,4},{1,5},{2,6},{3,7},{12,8},{13,9},{14,... | collective-permute-start | bytes 491528 | tf_op jit(solution)/shard_map/ppermute | solution.py:48
  143.2 25.7 %collective-permute-start.14 = (bf16[128,640]{1,0:T(8,128)(2,1)S(1)}, bf16[128,640]{1,0:T(8,128)(2,1)S(1)}, u32[]{:S(2)}, u32[]{:S(2)}) collective-permute-start(bf16[128,640]{1,0:T(8,128)(2,1)S(1)} %get-tuple-element.54), channel_id=1, source_target_pairs={{6,0},{7,1},{0,2},{1,3},{2,4},{3,5},{4,6},{5,7},{14,8},{15,9},{8,1... | collective-permute-start | bytes 491528 | tf_op jit(solution)/shard_map/ppermute | solution.py:48
  169.4 7.9 %collective-permute-start.19 = (bf16[4,128,640]{2,1,0:T(8,128)(2,1)S(1)}, bf16[4,128,640]{2,1,0:T(8,128)(2,1)S(1)}, u32[]{:S(2)}, u32[]{:S(2)}) collective-permute-start(bf16[4,128,640]{2,1,0:T(8,128)(2,1)S(1)} %shard_map.99), channel_id=1, source_target_pairs={{0,1},{1,0},{2,3},{3,2},{4,5},{5,4},{6,7},{7,6},{8,9},{9,8},{10,11... | collective-permute-start | bytes 1966088 | tf_op jit(solution)/shard_map/ppermute | solution.py:48
  172.4 3.5 %collective-permute-start.15 = (bf16[4,64,640]{2,1,0:T(8,128)(2,1)S(1)}, bf16[4,64,640]{2,1,0:T(8,128)(2,1)S(1)}, u32[]{:S(2)}, u32[]{:S(2)}) collective-permute-start(bf16[4,64,640]{2,1,0:T(8,128)(2,1)S(1)} %shard_map.97), channel_id=1, source_target_pairs={{0,1},{1,0},{2,3},{3,2},{4,5},{5,4},{6,7},{7,6},{8,9},{9,8},{10,11... | collective-permute-start | bytes 983048 | tf_op jit(solution)/shard_map/ppermute | solution.py:48
